TPU v7x, 32 devices: a whole 2x2x4 slice. The times are simulated.
32 devices in a mesh: grp: 4 (over y, x), wide: 8 (over z, core).
Axes of the slice: x: 2, y: 2, z: 4, core: 2. Of those that a mesh axis runs over, the one named last changes fastest.
Arguments:
- tiles: bfloat16 [1536, 256, 256], P(('grp', 'wide')), may hold values from -0.59765625 to 0.59765625
- contraction: int32 [1536], P(('grp', 'wide')), may hold values from 0 to 15
- row_tile: int32 [1536], P(('grp', 'wide')), may hold values from 0 to 31, as said below
- owner_map: int32 [32], replicated, may hold values from 0 to 31, as said below
- panel: bfloat16 [4096, 768], P('grp'), may hold values from -0.5390625 to 0.5390625
Outputs:
- column_block: float32 [8192, 768], P('wide')
Inputs may be any that keep to these rules, and one draw needn't show every extreme that they name: `row_tile`: every row tile's owner is owner_map // 4; among the 48 contributions of one device at most 16 have row tiles of one owner, and on every device some owner gets exactly 16. `owner_map`: A permutation of the row tiles.
All inputs are finite; a program needn't handle non-finite values.
Results may differ from a plain program's by a relative error of at most 0.0003.
Values may be sent and summed in bfloat16 or wider, within the bound.
No kernel may reach another device: no remote copies, remote signals or barrier semaphores. Data moves between devices by JAX's collectives and lax.ppermute only.
A program may use at most 192 MiB of HBM per device.

v0:
```python
import functools
import math

import jax
import jax.numpy as jnp
from jax import lax
from jax.experimental import pallas as pl
from jax.experimental.pallas import tpu as pltpu
from jax.sharding import PartitionSpec as P

MIB = 1024 * 1024
CODE_ROWS = 16
CODE_STEPS = 256.0
TOP = 32000.0
CHUNK = 256
UNROLL = 4
LOG2 = math.log(2.0)


def place_slots(row_ids, owner_map, out_dev):
    table_ids = jnp.arange(owner_map.shape[0], dtype=jnp.int32)
    position = jnp.sum(jnp.where(row_ids[..., None] == table_ids, owner_map, 0), axis=-1)
    target = position // out_dev
    serial = jnp.arange(row_ids.shape[-1], dtype=jnp.int32)
    earlier = (target[..., :, None] == target[..., None, :]) & (serial[:, None] > serial[None, :])
    ranking = jnp.sum(earlier.astype(jnp.int32), axis=-1)
    return (position % out_dev, target, ranking)


def add_products(summed, arrived, slot_labels, panel_tiles):
    slot_count = arrived.shape[0]
    block_rows = math.gcd(slot_count, 32)
    out_dev = summed.shape[0]
    local_ids = jnp.arange(out_dev, dtype=jnp.int32)

    def one_block(which_block, running, source_tiles, source_labels):
        part_tiles = lax.dynamic_slice_in_dim(source_tiles, which_block * block_rows, block_rows, 0)
        part_labels = lax.dynamic_slice_in_dim(
            source_labels, which_block * block_rows, block_rows, 0
        )
        chosen = jnp.take(panel_tiles, part_labels[:, 1], axis=0)
        products = jnp.einsum(
            "sab,sbc->sac", part_tiles, chosen, preferred_element_type=jnp.float32
        )
        row_hits = (part_labels[:, 0][:, None] == local_ids[None, :]).astype(jnp.float32)
        return running + jnp.einsum(
            "sr,sac->rac", row_hits, products, precision=lax.Precision.HIGHEST
        )

    return lax.fori_loop(
        0,
        slot_count // block_rows,
        lambda which_block, running: one_block(which_block, running, arrived, slot_labels),
        summed,
    )


def slots_plan(tiles, contraction, row_tile, owner_map, panel):
    wide_count = lax.axis_size("wide")
    tile_dev = tiles.shape[0]
    tile_side = tiles.shape[1]
    out_dev = owner_map.shape[0] // wide_count
    most_slots = tile_dev * 8 // (3 * wide_count)
    slot_total = wide_count * most_slots
    local_row, target, ranking = place_slots(row_tile, owner_map, out_dev)
    slot_index = target * most_slots + ranking
    outgoing = jnp.zeros((slot_total, tile_side, tile_side), tiles.dtype).at[slot_index].set(tiles)
    all_rows, all_contraction = (
        lax.all_gather(row_tile, "wide", axis=0, tiled=True),
        lax.all_gather(contraction, "wide", axis=0, tiled=True),
    )
    all_rows = all_rows.reshape(wide_count, tile_dev)
    all_contraction = all_contraction.reshape(wide_count, tile_dev)
    source_local, source_target, source_rank = place_slots(all_rows, owner_map, out_dev)
    source_ids = jnp.arange(wide_count, dtype=jnp.int32)
    mine = source_target == lax.axis_index("wide")
    arrive_index = jnp.where(mine, source_ids[:, None] * most_slots + source_rank, slot_total)
    label_pairs = jnp.stack([source_local, all_contraction], axis=-1).reshape(
        wide_count * tile_dev, 2
    )
    vacant_label = jnp.stack(
        [jnp.full((slot_total,), out_dev, jnp.int32), jnp.zeros((slot_total,), jnp.int32)], axis=1
    )
    arrived_labels = vacant_label.at[arrive_index.reshape(-1)].set(label_pairs, mode="drop")
    gathered = lax.all_gather(panel, "grp", axis=0, tiled=True)
    panel_tiles = gathered.reshape(gathered.shape[0] // tile_side, tile_side, gathered.shape[1])
    summed = jnp.zeros((out_dev, tile_side, gathered.shape[1]), jnp.float32)
    arrived = lax.all_to_all(outgoing, "wide", split_axis=0, concat_axis=0, tiled=True)
    summed = add_products(summed, arrived, arrived_labels, panel_tiles)
    summed = lax.psum(summed, "grp")
    return summed.reshape(out_dev * tile_side, gathered.shape[1])


def encode(value):
    largest = jnp.max(jnp.abs(value), axis=0, keepdims=True)
    code = jnp.ceil(jnp.log(jnp.maximum(largest, 1e-30)) * (CODE_STEPS / LOG2))
    scale = jnp.exp(code * (-LOG2 / CODE_STEPS)) * TOP
    whole = jnp.round(value * scale).astype(jnp.int32).astype(jnp.int16)
    return whole, code.astype(jnp.int32)


def put_encoded(ref, value):
    side = value.shape[0]
    whole, code = encode(value)
    ref[pl.ds(0, side), :] = whole
    ref[pl.ds(side, CODE_ROWS), :] = jnp.broadcast_to(
        code, (CODE_ROWS, code.shape[1])
    ).astype(jnp.int16)


def get_decoded(ref, side):
    code = ref[pl.ds(side, CODE_ROWS), :].astype(jnp.int32).astype(jnp.float32)[:1]
    scale = jnp.exp(code * (LOG2 / CODE_STEPS)) * (1.0 / TOP)
    return ref[pl.ds(0, side), :].astype(jnp.int32).astype(jnp.float32) * scale


def join_kernel(order_ref, *refs):
    *parts, out = refs
    rows = parts[0].shape[0]
    for i, part in enumerate(parts):
        out[pl.ds(i * rows, rows), :] = part[...]


def products_kernel(
    pieces, ends_ref, source_ref, slot_ref, label_ref, own_tiles, sib_tiles, *refs
):
    own_panel, near, far, *outs, held, stack, acc, sems = refs
    tile_dev, side = held.shape[1], held.shape[2]
    shard = own_panel.shape[0] // side
    half = shard // 2
    copies = []
    for q, (which, first, count) in enumerate(pieces):
        tiles = (own_tiles, sib_tiles)[which]
        copies.append(
            pltpu.make_async_copy(
                tiles.at[pl.ds(first, count)], held.at[which, pl.ds(first, count)], sems.at[q]
            )
        )
        copies[-1].start()
    for t in range(shard):
        stack[t] = own_panel[pl.ds(t * side, side), :]
    for i in range(3 * half):
        at = shard + (i // half) * shard + i % half
        stack[at] = near[pl.ds(i * side, side), :]
        stack[at + half] = far[pl.ds(i * side, side), :]

    @pl.loop(0, acc.shape[0])
    def _(i):
        acc[i] = jnp.zeros(acc.shape[1:], jnp.float32)

    def some(which, at, count):
        found = [
            jnp.dot(
                held[which, source_ref[which, at + u]],
                stack[label_ref[which, at + u]],
                preferred_element_type=jnp.float32,
            )
            for u in range(count)
        ]
        for u in range(count):
            acc[slot_ref[which, at + u]] += found[u]

    for q, (which, first, count) in enumerate(pieces):
        copies[q].wait()
        begin = 0 if first == 0 else ends_ref[q - 1]
        end = ends_ref[q]
        rounds = (end - begin) // UNROLL

        @pl.loop(0, rounds)
        def _(i, which=which, begin=begin):
            some(which, begin + i * UNROLL, UNROLL)

        @pl.loop(begin + rounds * UNROLL, end)
        def _(i, which=which):
            some(which, i, 1)

    sent = 0
    for out in outs:

        @pl.loop(0, out.shape[0])
        def _(i, out=out, sent=sent):
            if out.dtype == jnp.int16:
                put_encoded(out.at[i], acc[sent + i])
            else:
                out[i] = acc[sent + i]

        sent += out.shape[0]


def plane_kernel(bits_ref, recv_a, recv_b, kept, send_a, send_b, keep):
    side, half = kept.shape[1], send_a.shape[0]
    for first, bit, recv, send in ((0, bits_ref[1], recv_a, send_a), (1, bits_ref[0], recv_b, send_b)):

        @pl.loop(0, half)
        def _(i, first=first, bit=bit, recv=recv, send=send):
            other, mine = 2 * i + 1 - bit, 2 * i + bit
            base = first * 2 * half
            put_encoded(send.at[i], kept[base + other] + get_decoded(recv.at[other], side))
            keep[first * half + i] = kept[base + mine] + get_decoded(recv.at[mine], side)


def owner_kernel(bits_ref, recv_a, recv_b, kept, send, keep):
    side, half = kept.shape[1], send.shape[0]
    odd = bits_ref[2]

    @pl.loop(0, half)
    def _(i):
        value_a = kept[i] + get_decoded(recv_a.at[i], side)
        value_b = kept[half + i] + get_decoded(recv_b.at[i], side)
        put_encoded(send.at[i], jnp.where(odd == 1, value_a, value_b))
        keep[i] = jnp.where(odd == 1, value_b, value_a)


def line_kernel(bits_ref, recv, kept, send, keep):
    side, half = kept.shape[1], send.shape[0]
    bit = bits_ref[3]

    @pl.loop(0, half)
    def _(i):
        other, mine = (1 - bit) * half + i, bit * half + i
        put_encoded(send.at[i], kept[other] + get_decoded(recv.at[other], side))
        keep[i] = kept[mine] + get_decoded(recv.at[mine], side)


def rows_kernel(bits_ref, recv, kept, send_1, send_2, send_3, keep):
    side = kept.shape[1]
    row = bits_ref[1] * 2 + bits_ref[0]
    for d, send in enumerate((send_1, send_2, send_3), 1):
        put_encoded(send, kept[row ^ d] + get_decoded(recv.at[row ^ d], side))
    keep[...] = kept[row] + get_decoded(recv.at[row], side)


def finish_kernel(bits_ref, *refs):
    *recvs, kept, out = refs
    value = kept[...]
    for recv in recvs:
        value += get_decoded(recv, kept.shape[0])
    put_encoded(out, value)


def spread_kernel(bits_ref, *refs):
    blocks, out = refs[:4], refs[-1]
    side = blocks[0].shape[0] - CODE_ROWS
    row = bits_ref[1] * 2 + bits_ref[0]
    for d, block in enumerate(blocks):
        at = pl.multiple_of((row ^ d) * side, side)
        out[pl.ds(at, side), :] = get_decoded(block, side)


def in_vmem(count):
    return [pl.BlockSpec(memory_space=pltpu.VMEM)] * count


def in_smem(count):
    return [pl.BlockSpec(memory_space=pltpu.SMEM)] * count


def in_any(count):
    return [pl.BlockSpec(memory_space=pl.ANY)] * count


def shape(dims, kind):
    return jax.ShapeDtypeStruct(dims, kind)


def params(mib):
    return pltpu.CompilerParams(vmem_limit_bytes=mib * MIB)


def cost(flops, moved):
    return pl.CostEstimate(flops=flops, bytes_accessed=moved, transcendentals=0)


def compact(match, values):
    count = match.shape[-1]
    rank = jnp.cumsum(match.astype(jnp.int32), axis=-1) - 1
    at = jnp.arange(count, dtype=jnp.int32)
    hit = match[:, None, :] & (rank[:, None, :] == at[None, :, None])
    return [jnp.sum(jnp.where(hit, v[:, None, :], 0), axis=-1) for v in values]


def sums_plan(tiles, contraction, row_tile, owner_map, panel):
    wide_count = lax.axis_size("wide")
    tile_dev, side = tiles.shape[0], tiles.shape[1]
    out_dev = owner_map.shape[0] // wide_count
    rows, columns = panel.shape
    shard = rows // side
    chunks = columns // CHUNK
    sums = owner_map.shape[0] // 2
    g, w = lax.axis_index("grp"), lax.axis_index("wide")
    core = w % 2

    def to_core(v):
        return lax.ppermute(v, "wide", [(i, i ^ 1) for i in range(wide_count)])

    def to_grp(v, d):
        return lax.ppermute(v, "grp", [(i, i ^ d) for i in range(4)])

    def to_line(v, b):
        return lax.ppermute(v, "wide", [(i, i ^ (2 << b)) for i in range(wide_count)])

    x, y, z = g % 2, g // 2, w // 2
    bits = jnp.stack([x, y, z % 2, z // 2]).astype(jnp.int32)

    labels = jnp.stack([row_tile, contraction])
    both = jnp.stack([labels, to_core(labels)])
    sib_tiles = to_core(tiles)

    mines = [
        lax.dynamic_slice(panel, (core * (rows // 2), j * CHUNK), (rows // 2, CHUNK))
        for j in range(chunks)
    ]
    near = [[to_grp(mines[0], d) for d in (1, 2, 3)]]
    for mine in mines[1:]:
        mine = lax.optimization_barrier((mine, *near[-1]))[0]
        near.append([to_grp(mine, d) for d in (1, 2, 3)])

    table_ids = jnp.arange(owner_map.shape[0], dtype=jnp.int32)
    position = jnp.sum(jnp.where(both[:, 0, :, None] == table_ids, owner_map, 0), axis=-1)
    owner, local = position // out_dev, position % out_dev
    to_z, odd = owner // 4, (owner // 2) % 2
    bit_x, bit_y = local % 2, local // 2
    first = jnp.where(odd == 1, bit_y == y, bit_x == x)
    second = jnp.where(odd == 1, bit_x, bit_y)
    in_plane = jnp.where(first, sums // 2, 0) + odd * (sums // 4) + 2 * to_z + second
    in_line = jnp.where(odd == z % 2, sums // 2, 0) + to_z * out_dev + local
    k = both[:, 1]
    apart, inner = (k // shard) ^ g, k % shard
    half = shard // 2
    crossed = jnp.where(inner // half == core, 0, half) + inner % half
    label = jnp.where(apart == 0, inner, apart * shard + crossed)
    match = owner % 2 == core
    serial = jnp.broadcast_to(jnp.arange(tile_dev, dtype=jnp.int32), match.shape)
    source, in_plane, in_line, label = compact(match, [serial, in_plane, in_line, label])
    cut = tile_dev // 4
    pieces = ((0, 0, cut), (0, cut, tile_dev - cut), (1, 0, tile_dev))
    ends = jnp.stack(
        [
            jnp.sum((match[which] & (serial[which] < first + count)).astype(jnp.int32))
            for which, first, count in pieces
        ]
    )

    half, quarter = sums // 2, sums // 4
    coded = shape((side + CODE_ROWS, CHUNK), jnp.int16)
    plain = shape((side, CHUNK), jnp.float32)

    def stack_of(count, one):
        return shape((count, *one.shape), one.dtype)

    last = None

    def in_order(small):
        return small if last is None else lax.optimization_barrier((small, last))[0]

    def call(body, name, outs, *args):
        nonlocal last
        done = pl.pallas_call(
            body,
            in_specs=in_smem(1) + in_vmem(len(args)),
            out_specs=in_vmem(len(outs)),
            out_shape=outs,
            compiler_params=params(16),
            cost_estimate=cost(0, sum(math.prod(a.shape) * a.dtype.itemsize for a in args)),
            name=name,
        )(in_order(bits), *args)
        last = done[0]
        return done

    def join(j):
        (joined,) = call(join_kernel, "join", [shape((3 * rows // 2, CHUNK), panel.dtype)], *near[j])
        return joined, to_core(joined)

    def products(j, slot, outs, joined, crossed):
        nonlocal last
        done = pl.pallas_call(
            functools.partial(products_kernel, pieces),
            grid=(1,),
            in_specs=in_smem(4)
            + [pl.BlockSpec(memory_space=pltpu.HBM)] * 2
            + [pl.BlockSpec((rows, CHUNK), lambda i: (0, j))]
            + in_vmem(2),
            out_specs=in_vmem(len(outs)),
            out_shape=outs,
            scratch_shapes=[
                pltpu.VMEM((2, tile_dev, side, side), tiles.dtype),
                pltpu.VMEM((4 * shard, side, CHUNK), panel.dtype),
                pltpu.VMEM((sums, side, CHUNK), jnp.float32),
                pltpu.SemaphoreType.DMA((len(pieces),)),
            ],
            compiler_params=params(54),
            cost_estimate=cost(0, 4 * tile_dev * side * side),
            name="products",
        )(in_order(ends), source, slot, label, tiles, sib_tiles, panel, joined, crossed)
        last = done[0]
        return done

    def spread(j, done, result):
        nonlocal last
        blocks = [done] + [to_grp(done, d) for d in (1, 2, 3)]
        earlier = [] if result is None else [result]
        last = pl.pallas_call(
            spread_kernel,
            grid=(1,),
            in_specs=in_smem(1) + in_vmem(4) + in_any(len(earlier)),
            out_specs=pl.BlockSpec((out_dev * side, CHUNK), lambda i: (0, j)),
            out_shape=shape((out_dev * side, columns), jnp.float32),
            input_output_aliases={5: 0} if earlier else {},
            compiler_params=params(16),
            cost_estimate=cost(0, 6 * out_dev * side * CHUNK),
            name="spread",
        )(in_order(bits), *blocks, *earlier)
        return last

    def line_first(j):
        joined, crossed = join(j)
        yield
        send, keep = products(
            j, in_line, [stack_of(half, coded), stack_of(half, plain)], joined, crossed
        )
        yield
        recv = to_line(send, 0)
        send, keep = call(
            line_kernel, "line", [stack_of(quarter, coded), stack_of(quarter, plain)], recv, keep
        )
        yield
        *sends, keep = call(rows_kernel, "rows", [coded] * 3 + [plain], to_line(send, 1), keep)
        yield
        recvs = [to_grp(v, d) for d, v in enumerate(sends, 1)]
        (done,) = call(finish_kernel, "finish", [coded], *recvs, keep)
        yield
        yield done

    def plane_first(j):
        joined, crossed = join(j)
        yield
        send_a, send_b, keep = products(
            j, in_plane, [stack_of(quarter, coded)] * 2 + [stack_of(half, plain)], joined, crossed
        )
        yield
        send_a, send_b, keep = call(
            plane_kernel,
            "plane",
            [stack_of(quarter // 2, coded)] * 2 + [stack_of(quarter, plain)],
            to_grp(send_a, 1),
            to_grp(send_b, 2),
            keep,
        )
        yield
        send, keep = call(
            owner_kernel,
            "owner",
            [stack_of(quarter // 2, coded), stack_of(quarter // 2, plain)],
            to_grp(send_a, 2),
            to_grp(send_b, 1),
            keep,
        )
        yield
        send, keep = call(
            line_kernel,
            "line",
            [stack_of(quarter // 4, coded), stack_of(quarter // 4, plain)],
            to_line(send, 0),
            keep,
        )
        yield
        recv = to_line(send, 1)
        (done,) = call(finish_kernel, "finish", [coded], recv[0], keep[0])
        yield
        yield done

    steps, lengths = [0] * chunks, [5] + [6] * (chunks - 1)
    work = [(line_first if j == 0 else plane_first)(j) for j in range(chunks)]
    dones, result = {}, None
    for j in (0, 0, 1, 1, 2, 2, 0, 1, 2, 1, 0, 2, 1, 0, 1, 2, 0, 2, 1, 2):
        if j in dones:
            result = spread(j, dones[j], result)
            continue
        next(work[j])
        steps[j] += 1
        if steps[j] == lengths[j]:
            dones[j] = next(work[j])
    return result


def per_device(tiles, contraction, row_tile, owner_map, panel):
    dense = owner_map.shape[0] <= tiles.shape[0]
    wide_count = lax.axis_size("wide")
    fits = lax.axis_size("grp") == 4 and wide_count >= 4 and wide_count & (wide_count - 1) == 0
    out_dev = owner_map.shape[0] // wide_count
    if dense and fits and wide_count == 8 and out_dev == 4 and panel.shape[1] == 3 * CHUNK:
        return sums_plan(tiles, contraction, row_tile, owner_map, panel)
    return slots_plan(tiles, contraction, row_tile, owner_map, panel)


def solution(mesh):
    return jax.shard_map(
        per_device,
        mesh=mesh,
        in_specs=(
            P(("grp", "wide"), None, None),
            P(("grp", "wide")),
            P(("grp", "wide")),
            P(),
            P("grp", None),
        ),
        out_specs=P("wide", None),
        check_vma=False,
    )
```

profile of v0, /device:TPU:0, one launch (start us, length us, event | category | flops | bytes accessed | tf_op | source)
XLA Modules:
  0.0 142.1 jit_solution(9480221067300945330)
XLA Ops:
  1.6 3.5 %collective-permute-start.3 = (bf16[512,256]{1,0:T(8,128)(2,1)S(1)}, bf16[512,256]{1,0:T(8,128)(2,1)S(1)}, u32[]{:S(2)}, u32[]{:S(2)}) collective-permute-start(bf16[512,256]{1,0:T(8,128)(2,1)S(1)} %get-tuple-element.117), channel_id=1, source_target_pairs={{0,24},{8,16},{16,8},{24,0},{1,25},{9,17},{17,9},{25,1},{2,26},{10... | collective-permute-start | bytes 786440 | tf_op jit(solution)/shard_map/ppermute | solution.py:297
  6.6 3.6 %collective-permute-done = s32[2,48]{1,0:T(2,128)S(1)} collective-permute-done((s32[2,48]{1,0:T(2,128)S(1)}, s32[2,48]{1,0:T(2,128)S(1)}, u32[]{:S(2)}, u32[]{:S(2)}) %collective-permute-start) | collective-permute-done | bytes 416 | tf_op jit(solution)/shard_map/ppermute | solution.py:294
  12.3 5.4 %collective-permute-done.2.refs_1_ = bf16[512,256]{1,0:T(8,128)(2,1)S(1)} collective-permute-done((bf16[512,256]{1,0:T(8,128)(2,1)S(1)}, bf16[512,256]{1,0:T(8,128)(2,1)S(1)}, u32[]{:S(2)}, u32[]{:S(2)}) %collective-permute-start.2) | collective-permute-done | bytes 262176 | tf_op jit(solution)/shard_map/ppermute | solution.py:297
  23.2 2.4 %pad_add_fusion.3.ends_ref = s32[3]{0:T(128)} fusion(s32[1]{0:T(128)} %bitcast.11, s32[1]{0:T(128)} %bitcast.10, s32[1]{0:T(128)} %bitcast.9), kind=kLoop, calls=%fused_computation.62 | loop fusion | flops 6 | bytes 24 | tf_op jit(solution)/shard_map/stack | solution.py:337
  27.4 12.1 %products.3 = (s16[8,272,256]{2,1,0:T(8,128)(2,1)}, f32[8,256,256]{2,1,0:T(8,128)}) custom-call(s32[3]{0:T(128)} %pad_add_fusion.3.ends_ref, s32[2,48]{1,0:T(2,128)} %get-tuple-element.106.source_ref, s32[2,48]{1,0:T(2,128)} %get-tuple-element.105.slot_ref, s32[2,48]{1,0:T(2,128)} %get-tuple-element.104.label_ref, bf16[48,256,256]{2,1,0:T(8,128)(2,1)} %own_tiles.5, ...), custom_call_target="tpu_custom_call" | custom-call | bytes 12582912 | tf_op jit(solution)/shard_map/products/pallas_call | solution.py:376
  41.6 2.4 %collective-permute-start.11 = (bf16[512,256]{1,0:T(8,128)(2,1)S(1)}, bf16[512,256]{1,0:T(8,128)(2,1)S(1)}, u32[]{:S(2)}, u32[]{:S(2)}) collective-permute-start(bf16[512,256]{1,0:T(8,128)(2,1)S(1)} %get-tuple-element.61), channel_id=1, source_target_pairs={{0,16},{8,24},{16,0},{24,8},{1,17},{9,25},{17,1},{25,9},{2,18},{10... | collective-permute-start | bytes 786440 | tf_op jit(solution)/shard_map/ppermute | solution.py:297
  46.0 12.1 %products.4 = (s16[4,272,256]{2,1,0:T(8,128)(2,1)}, s16[4,272,256]{2,1,0:T(8,128)(2,1)}, f32[8,256,256]{2,1,0:T(8,128)}) custom-call(s32[3]{0:T(128)} %pad_add_fusion.3.ends_ref, s32[2,48]{1,0:T(2,128)} %get-tuple-element.106.source_ref, s32[2,48]{1,0:T(2,128)} %get-tuple-element.103.slot_ref, s32[2,48]{1,0:T(2,128)} %get-tuple-element.104.label_ref, ...), custom_call_target="tpu_custom_call" | custom-call | bytes 12582912 | tf_op jit(solution)/shard_map/products/pallas_call | solution.py:376
  58.8 3.1 %collective-permute-start.16 = (s16[4,272,256]{2,1,0:T(8,128)(2,1)}, s16[4,272,256]{2,1,0:T(8,128)(2,1)S(1)}, u32[]{:S(2)}, u32[]{:S(2)}) collective-permute-start(s16[4,272,256]{2,1,0:T(8,128)(2,1)} %get-tuple-element.68), channel_id=1, source_target_pairs={{0,16},{8,24},{16,0},{24,8},{1,17},{9,25},{17,1},{25,9},{2,18},{10... | collective-permute-start | bytes 1671176 | tf_op jit(solution)/shard_map/ppermute | solution.py:297
  62.9 12.0 %products.5 = (s16[4,272,256]{2,1,0:T(8,128)(2,1)}, s16[4,272,256]{2,1,0:T(8,128)(2,1)}, f32[8,256,256]{2,1,0:T(8,128)}) custom-call(s32[3]{0:T(128)} %pad_add_fusion.3.ends_ref, s32[2,48]{1,0:T(2,128)} %get-tuple-element.106.source_ref, s32[2,48]{1,0:T(2,128)} %get-tuple-element.103.slot_ref, s32[2,48]{1,0:T(2,128)} %get-tuple-element.104.label_ref, ...), custom_call_target="tpu_custom_call" | custom-call | bytes 12582912 | tf_op jit(solution)/shard_map/products/pallas_call | solution.py:376
  75.0 3.5 %collective-permute-start.18 = (s16[4,272,256]{2,1,0:T(8,128)(2,1)}, s16[4,272,256]{2,1,0:T(8,128)(2,1)S(1)}, u32[]{:S(2)}, u32[]{:S(2)}) collective-permute-start(s16[4,272,256]{2,1,0:T(8,128)(2,1)} %get-tuple-element.72), channel_id=1, source_target_pairs={{0,16},{8,24},{16,0},{24,8},{1,17},{9,25},{17,1},{25,9},{2,18},{10... | collective-permute-start | bytes 1671176 | tf_op jit(solution)/shard_map/ppermute | solution.py:297
  79.7 4.2 %collective-permute-start.21 = (s16[4,272,256]{2,1,0:T(8,128)(2,1)S(1)}, s16[4,272,256]{2,1,0:T(8,128)(2,1)S(1)}, u32[]{:S(2)}, u32[]{:S(2)}) collective-permute-start(s16[4,272,256]{2,1,0:T(8,128)(2,1)S(1)} %get-tuple-element.66), channel_id=1, source_target_pairs={{0,4},{1,5},{2,6},{3,7},{4,0},{5,1},{6,2},{7,3},{8,12},{9,13},{10,... | collective-permute-start | bytes 1671176 | tf_op jit(solution)/shard_map/ppermute | solution.py:300
  87.1 5.1 %collective-permute-done.18.recv_b = s16[4,272,256]{2,1,0:T(8,128)(2,1)S(1)} collective-permute-done((s16[4,272,256]{2,1,0:T(8,128)(2,1)}, s16[4,272,256]{2,1,0:T(8,128)(2,1)S(1)}, u32[]{:S(2)}, u32[]{:S(2)}) %collective-permute-start.18) | collective-permute-done | bytes 557088 | tf_op jit(solution)/shard_map/ppermute | solution.py:297
  92.2 2.0 %collective-permute-done.17.recv_a = s16[4,272,256]{2,1,0:T(8,128)(2,1)S(1)} collective-permute-done((s16[4,272,256]{2,1,0:T(8,128)(2,1)}, s16[4,272,256]{2,1,0:T(8,128)(2,1)S(1)}, u32[]{:S(2)}, u32[]{:S(2)}) %collective-permute-start.17) | collective-permute-done | bytes 557088 | tf_op jit(solution)/shard_map/ppermute | solution.py:297
  99.2 5.4 %collective-permute-done.21.recv = s16[4,272,256]{2,1,0:T(8,128)(2,1)S(1)} collective-permute-done((s16[4,272,256]{2,1,0:T(8,128)(2,1)S(1)}, s16[4,272,256]{2,1,0:T(8,128)(2,1)S(1)}, u32[]{:S(2)}, u32[]{:S(2)}) %collective-permute-start.21) | collective-permute-done | bytes 557088 | tf_op jit(solution)/shard_map/ppermute | solution.py:300
  108.2 1.7 %collective-permute-start.25 = (s16[272,256]{1,0:T(8,128)(2,1)S(1)}, s16[272,256]{1,0:T(8,128)(2,1)S(1)}, u32[]{:S(2)}, u32[]{:S(2)}) collective-permute-start(s16[272,256]{1,0:T(8,128)(2,1)S(1)} %get-tuple-element.81), channel_id=1, source_target_pairs={{0,8},{8,0},{16,24},{24,16},{1,9},{9,1},{17,25},{25,17},{2,10},{10... | collective-permute-start | bytes 417800 | tf_op jit(solution)/shard_map/ppermute | solution.py:297
  111.2 2.6 %collective-permute-start.28 = (s16[1,272,256]{2,1,0:T(8,128)(2,1)S(1)}, s16[1,272,256]{2,1,0:T(8,128)(2,1)S(1)}, u32[]{:S(2)}, u32[]{:S(2)}) collective-permute-start(s16[1,272,256]{2,1,0:T(8,128)(2,1)S(1)} %get-tuple-element.88), channel_id=1, source_target_pairs={{0,4},{1,5},{2,6},{3,7},{4,0},{5,1},{6,2},{7,3},{8,12},{9,13},{10,... | collective-permute-start | bytes 417800 | tf_op jit(solution)/shard_map/ppermute | solution.py:300
  118.5 1.9 %collective-permute-start.30 = (s16[272,256]{1,0:T(8,128)(2,1)S(1)}, s16[272,256]{1,0:T(8,128)(2,1)S(1)}, u32[]{:S(2)}, u32[]{:S(2)}) collective-permute-start(s16[272,256]{1,0:T(8,128)(2,1)S(1)} %finish.3.refs_0_), channel_id=1, source_target_pairs={{0,8},{8,0},{16,24},{24,16},{1,9},{9,1},{17,25},{25,17},{2,10},{10... | collective-permute-start | bytes 417800 | tf_op jit(solution)/shard_map/ppermute | solution.py:297
  122.0 2.3 %collective-permute-start.33 = (s16[1,272,256]{2,1,0:T(8,128)(2,1)S(1)}, s16[1,272,256]{2,1,0:T(8,128)(2,1)S(1)}, u32[]{:S(2)}, u32[]{:S(2)}) collective-permute-start(s16[1,272,256]{2,1,0:T(8,128)(2,1)S(1)} %get-tuple-element.97), channel_id=1, source_target_pairs={{0,4},{1,5},{2,6},{3,7},{4,0},{5,1},{6,2},{7,3},{8,12},{9,13},{10,... | collective-permute-start | bytes 417800 | tf_op jit(solution)/shard_map/ppermute | solution.py:300
  127.8 1.6 %spread.3.refs_4_ = f32[1024,768]{1,0:T(8,128)} custom-call(s32[4]{0:T(128)S(1)} %pad_add_fusion.2.order_ref.bits_ref, s16[272,256]{1,0:T(8,128)(2,1)S(1)} %finish.3.refs_0_, s16[272,256]{1,0:T(8,128)(2,1)S(1)} %collective-permute-done.30.refs_1_, s16[272,256]{1,0:T(8,128)(2,1)S(1)} %collective-permute-done.31.refs_2_, ...), custom_call_target="tpu_custom_call" | custom-call | bytes 1572864 | tf_op jit(solution)/shard_map/spread/pallas_call | solution.py:402
  129.5 1.7 %collective-permute-done.33 = s16[1,272,256]{2,1,0:T(8,128)(2,1)S(1)} collective-permute-done((s16[1,272,256]{2,1,0:T(8,128)(2,1)S(1)}, s16[1,272,256]{2,1,0:T(8,128)(2,1)S(1)}, u32[]{:S(2)}, u32[]{:S(2)}) %collective-permute-start.33) | collective-permute-done | bytes 139296 | tf_op jit(solution)/shard_map/ppermute | solution.py:300
  133.4 1.9 %collective-permute-start.37 = (s16[272,256]{1,0:T(8,128)(2,1)S(1)}, s16[272,256]{1,0:T(8,128)(2,1)S(1)}, u32[]{:S(2)}, u32[]{:S(2)}) collective-permute-start(s16[272,256]{1,0:T(8,128)(2,1)S(1)} %finish.5.refs_0_), channel_id=1, source_target_pairs={{0,8},{8,0},{16,24},{24,16},{1,9},{9,1},{17,25},{25,17},{2,10},{10... | collective-permute-start | bytes 417800 | tf_op jit(solution)/shard_map/ppermute | solution.py:297
  135.3 1.6 %spread.4.refs_4_ = f32[1024,768]{1,0:T(8,128)} custom-call(s32[4]{0:T(128)S(1)} %pad_add_fusion.2.order_ref.bits_ref, s16[272,256]{1,0:T(8,128)(2,1)S(1)} %finish.4.refs_0_, s16[272,256]{1,0:T(8,128)(2,1)S(1)} %collective-permute-done.34.refs_1_, s16[272,256]{1,0:T(8,128)(2,1)S(1)} %collective-permute-done.35.refs_2_, ...), custom_call_target="tpu_custom_call", output_to_operand_aliasing={{}: (5, {})} | custom-call | bytes 1572864 | tf_op jit(solution)/shard_map/spread/pallas_call | solution.py:402
  136.9 2.4 %collective-permute-done.39.refs_3_ = s16[272,256]{1,0:T(8,128)(2,1)S(1)} collective-permute-done((s16[272,256]{1,0:T(8,128)(2,1)S(1)}, s16[272,256]{1,0:T(8,128)(2,1)S(1)}, u32[]{:S(2)}, u32[]{:S(2)}) %collective-permute-start.39) | collective-permute-done | bytes 139296 | tf_op jit(solution)/shard_map/ppermute | solution.py:297
  140.5 1.6 %spread.5 = f32[1024,768]{1,0:T(8,128)} custom-call(s32[4]{0:T(128)S(1)} %pad_add_fusion.2.order_ref.bits_ref, s16[272,256]{1,0:T(8,128)(2,1)S(1)} %finish.5.refs_0_, s16[272,256]{1,0:T(8,128)(2,1)S(1)} %collective-permute-done.37.refs_1_, s16[272,256]{1,0:T(8,128)(2,1)S(1)} %collective-permute-done.38.refs_2_, ...), custom_call_target="tpu_custom_call", output_to_operand_aliasing={{}: (5, {})} | custom-call | bytes 1572864 | tf_op jit(solution)/shard_map/spread/pallas_call | solution.py:402
  (108 shorter events, 45.4 us)
Async XLA Ops:
  0.0 26.4 %collective-permute-start.4 = (bf16[48,256,256]{2,1,0:T(8,128)(2,1)}, bf16[48,256,256]{2,1,0:T(8,128)(2,1)}, u32[]{:S(2)}, u32[]{:S(2)}) collective-permute-start(bf16[48,256,256]{2,1,0:T(8,128)(2,1)} %own_tiles.5), channel_id=1, source_target_pairs={{0,1},{1,0},{2,3},{3,2},{4,5},{5,4},{6,7},{7,6},{8,9},{9,8},{10,11... | collective-permute-start | bytes 18874376 | tf_op jit(solution)/shard_map/ppermute | solution.py:294
  1.6 10.7 %collective-permute-start.3 = (bf16[512,256]{1,0:T(8,128)(2,1)S(1)}, bf16[512,256]{1,0:T(8,128)(2,1)S(1)}, u32[]{:S(2)}, u32[]{:S(2)}) collective-permute-start(bf16[512,256]{1,0:T(8,128)(2,1)S(1)} %get-tuple-element.117), channel_id=1, source_target_pairs={{0,24},{8,16},{16,8},{24,0},{1,25},{9,17},{17,9},{25,1},{2,26},{10... | collective-permute-start | bytes 786440 | tf_op jit(solution)/shard_map/ppermute | solution.py:297
  5.1 12.6 %collective-permute-start.2 = (bf16[512,256]{1,0:T(8,128)(2,1)S(1)}, bf16[512,256]{1,0:T(8,128)(2,1)S(1)}, u32[]{:S(2)}, u32[]{:S(2)}) collective-permute-start(bf16[512,256]{1,0:T(8,128)(2,1)S(1)} %get-tuple-element.117), channel_id=1, source_target_pairs={{0,16},{8,24},{16,0},{24,8},{1,17},{9,25},{17,1},{25,9},{2,18},{10... | collective-permute-start | bytes 786440 | tf_op jit(solution)/shard_map/ppermute | solution.py:297
  5.6 12.4 %collective-permute-start.1 = (bf16[512,256]{1,0:T(8,128)(2,1)S(1)}, bf16[512,256]{1,0:T(8,128)(2,1)S(1)}, u32[]{:S(2)}, u32[]{:S(2)}) collective-permute-start(bf16[512,256]{1,0:T(8,128)(2,1)S(1)} %get-tuple-element.117), channel_id=1, source_target_pairs={{0,8},{8,0},{16,24},{24,16},{1,9},{9,1},{17,25},{25,17},{2,10},{10... | collective-permute-start | bytes 786440 | tf_op jit(solution)/shard_map/ppermute | solution.py:297
  19.0 20.5 %collective-permute-start.8 = (bf16[512,256]{1,0:T(8,128)(2,1)S(1)}, bf16[512,256]{1,0:T(8,128)(2,1)S(1)}, u32[]{:S(2)}, u32[]{:S(2)}) collective-permute-start(bf16[512,256]{1,0:T(8,128)(2,1)S(1)} %get-tuple-element.57), channel_id=1, source_target_pairs={{0,24},{8,16},{16,8},{24,0},{1,25},{9,17},{17,9},{25,1},{2,26},{10... | collective-permute-start | bytes 786440 | tf_op jit(solution)/shard_map/ppermute | solution.py:297
  20.6 18.9 %collective-permute-start.7 = (bf16[512,256]{1,0:T(8,128)(2,1)S(1)}, bf16[512,256]{1,0:T(8,128)(2,1)S(1)}, u32[]{:S(2)}, u32[]{:S(2)}) collective-permute-start(bf16[512,256]{1,0:T(8,128)(2,1)S(1)} %get-tuple-element.57), channel_id=1, source_target_pairs={{0,16},{8,24},{16,0},{24,8},{1,17},{9,25},{17,1},{25,9},{2,18},{10... | collective-permute-start | bytes 786440 | tf_op jit(solution)/shard_map/ppermute | solution.py:297
  22.0 17.5 %collective-permute-start.6 = (bf16[512,256]{1,0:T(8,128)(2,1)S(1)}, bf16[512,256]{1,0:T(8,128)(2,1)S(1)}, u32[]{:S(2)}, u32[]{:S(2)}) collective-permute-start(bf16[512,256]{1,0:T(8,128)(2,1)S(1)} %get-tuple-element.57), channel_id=1, source_target_pairs={{0,8},{8,0},{16,24},{24,16},{1,9},{9,1},{17,25},{25,17},{2,10},{10... | collective-permute-start | bytes 786440 | tf_op jit(solution)/shard_map/ppermute | solution.py:297
  40.2 17.9 %collective-permute-start.12 = (bf16[512,256]{1,0:T(8,128)(2,1)S(1)}, bf16[512,256]{1,0:T(8,128)(2,1)S(1)}, u32[]{:S(2)}, u32[]{:S(2)}) collective-permute-start(bf16[512,256]{1,0:T(8,128)(2,1)S(1)} %get-tuple-element.61), channel_id=1, source_target_pairs={{0,24},{8,16},{16,8},{24,0},{1,25},{9,17},{17,9},{25,1},{2,26},{10... | collective-permute-start | bytes 786440 | tf_op jit(solution)/shard_map/ppermute | solution.py:297
  41.6 16.5 %collective-permute-start.11 = (bf16[512,256]{1,0:T(8,128)(2,1)S(1)}, bf16[512,256]{1,0:T(8,128)(2,1)S(1)}, u32[]{:S(2)}, u32[]{:S(2)}) collective-permute-start(bf16[512,256]{1,0:T(8,128)(2,1)S(1)} %get-tuple-element.61), channel_id=1, source_target_pairs={{0,16},{8,24},{16,0},{24,8},{1,17},{9,25},{17,1},{25,9},{2,18},{10... | collective-permute-start | bytes 786440 | tf_op jit(solution)/shard_map/ppermute | solution.py:297
  44.0 14.1 %collective-permute-start.10 = (bf16[512,256]{1,0:T(8,128)(2,1)S(1)}, bf16[512,256]{1,0:T(8,128)(2,1)S(1)}, u32[]{:S(2)}, u32[]{:S(2)}) collective-permute-start(bf16[512,256]{1,0:T(8,128)(2,1)S(1)} %get-tuple-element.61), channel_id=1, source_target_pairs={{0,8},{8,0},{16,24},{24,16},{1,9},{9,1},{17,25},{25,17},{2,10},{10... | collective-permute-start | bytes 786440 | tf_op jit(solution)/shard_map/ppermute | solution.py:297
  44.4 34.1 %collective-permute-start.14 = (s16[8,272,256]{2,1,0:T(8,128)(2,1)}, s16[8,272,256]{2,1,0:T(8,128)(2,1)S(1)}, u32[]{:S(2)}, u32[]{:S(2)}) collective-permute-start(s16[8,272,256]{2,1,0:T(8,128)(2,1)} %get-tuple-element.55), channel_id=1, source_target_pairs={{0,2},{1,3},{2,0},{3,1},{4,6},{5,7},{6,4},{7,5},{8,10},{9,11},{10,... | collective-permute-start | bytes 3342344 | tf_op jit(solution)/shard_map/ppermute | solution.py:300
  58.8 25.0 %collective-permute-start.16 = (s16[4,272,256]{2,1,0:T(8,128)(2,1)}, s16[4,272,256]{2,1,0:T(8,128)(2,1)S(1)}, u32[]{:S(2)}, u32[]{:S(2)}) collective-permute-start(s16[4,272,256]{2,1,0:T(8,128)(2,1)} %get-tuple-element.68), channel_id=1, source_target_pairs={{0,16},{8,24},{16,0},{24,8},{1,17},{9,25},{17,1},{25,9},{2,18},{10... | collective-permute-start | bytes 1671176 | tf_op jit(solution)/shard_map/ppermute | solution.py:297
  62.0 21.9 %collective-permute-start.15 = (s16[4,272,256]{2,1,0:T(8,128)(2,1)}, s16[4,272,256]{2,1,0:T(8,128)(2,1)S(1)}, u32[]{:S(2)}, u32[]{:S(2)}) collective-permute-start(s16[4,272,256]{2,1,0:T(8,128)(2,1)} %get-tuple-element.59), channel_id=1, source_target_pairs={{0,8},{8,0},{16,24},{24,16},{1,9},{9,1},{17,25},{25,17},{2,10},{10... | collective-permute-start | bytes 1671176 | tf_op jit(solution)/shard_map/ppermute | solution.py:297
  75.0 17.2 %collective-permute-start.18 = (s16[4,272,256]{2,1,0:T(8,128)(2,1)}, s16[4,272,256]{2,1,0:T(8,128)(2,1)S(1)}, u32[]{:S(2)}, u32[]{:S(2)}) collective-permute-start(s16[4,272,256]{2,1,0:T(8,128)(2,1)} %get-tuple-element.72), channel_id=1, source_target_pairs={{0,16},{8,24},{16,0},{24,8},{1,17},{9,25},{17,1},{25,9},{2,18},{10... | collective-permute-start | bytes 1671176 | tf_op jit(solution)/shard_map/ppermute | solution.py:297
  78.5 15.8 %collective-permute-start.17 = (s16[4,272,256]{2,1,0:T(8,128)(2,1)}, s16[4,272,256]{2,1,0:T(8,128)(2,1)S(1)}, u32[]{:S(2)}, u32[]{:S(2)}) collective-permute-start(s16[4,272,256]{2,1,0:T(8,128)(2,1)} %get-tuple-element.63), channel_id=1, source_target_pairs={{0,8},{8,0},{16,24},{24,16},{1,9},{9,1},{17,25},{25,17},{2,10},{10... | collective-permute-start | bytes 1671176 | tf_op jit(solution)/shard_map/ppermute | solution.py:297
  79.7 24.9 %collective-permute-start.21 = (s16[4,272,256]{2,1,0:T(8,128)(2,1)S(1)}, s16[4,272,256]{2,1,0:T(8,128)(2,1)S(1)}, u32[]{:S(2)}, u32[]{:S(2)}) collective-permute-start(s16[4,272,256]{2,1,0:T(8,128)(2,1)S(1)} %get-tuple-element.66), channel_id=1, source_target_pairs={{0,4},{1,5},{2,6},{3,7},{4,0},{5,1},{6,2},{7,3},{8,12},{9,13},{10,... | collective-permute-start | bytes 1671176 | tf_op jit(solution)/shard_map/ppermute | solution.py:300
  85.0 12.7 %collective-permute-start.20 = (s16[2,272,256]{2,1,0:T(8,128)(2,1)S(1)}, s16[2,272,256]{2,1,0:T(8,128)(2,1)S(1)}, u32[]{:S(2)}, u32[]{:S(2)}) collective-permute-start(s16[2,272,256]{2,1,0:T(8,128)(2,1)S(1)} %get-tuple-element.76), channel_id=1, source_target_pairs={{0,8},{8,0},{16,24},{24,16},{1,9},{9,1},{17,25},{25,17},{2,10},{10... | collective-permute-start | bytes 835592 | tf_op jit(solution)/shard_map/ppermute | solution.py:297
  85.5 12.3 %collective-permute-start.19 = (s16[2,272,256]{2,1,0:T(8,128)(2,1)S(1)}, s16[2,272,256]{2,1,0:T(8,128)(2,1)S(1)}, u32[]{:S(2)}, u32[]{:S(2)}) collective-permute-start(s16[2,272,256]{2,1,0:T(8,128)(2,1)S(1)} %get-tuple-element.70), channel_id=1, source_target_pairs={{0,16},{8,24},{16,0},{24,8},{1,17},{9,25},{17,1},{25,9},{2,18},{10... | collective-permute-start | bytes 835592 | tf_op jit(solution)/shard_map/ppermute | solution.py:297
  95.4 10.0 %collective-permute-start.23 = (s16[2,272,256]{2,1,0:T(8,128)(2,1)S(1)}, s16[2,272,256]{2,1,0:T(8,128)(2,1)S(1)}, u32[]{:S(2)}, u32[]{:S(2)}) collective-permute-start(s16[2,272,256]{2,1,0:T(8,128)(2,1)S(1)} %get-tuple-element.83), channel_id=1, source_target_pairs={{0,8},{8,0},{16,24},{24,16},{1,9},{9,1},{17,25},{25,17},{2,10},{10... | collective-permute-start | bytes 835592 | tf_op jit(solution)/shard_map/ppermute | solution.py:297
  95.5 9.9 %collective-permute-start.22 = (s16[2,272,256]{2,1,0:T(8,128)(2,1)S(1)}, s16[2,272,256]{2,1,0:T(8,128)(2,1)S(1)}, u32[]{:S(2)}, u32[]{:S(2)}) collective-permute-start(s16[2,272,256]{2,1,0:T(8,128)(2,1)S(1)} %get-tuple-element.74), channel_id=1, source_target_pairs={{0,16},{8,24},{16,0},{24,8},{1,17},{9,25},{17,1},{25,9},{2,18},{10... | collective-permute-start | bytes 835592 | tf_op jit(solution)/shard_map/ppermute | solution.py:297
  98.6 11.9 %collective-permute-start.24 = (s16[2,272,256]{2,1,0:T(8,128)(2,1)S(1)}, s16[2,272,256]{2,1,0:T(8,128)(2,1)S(1)}, u32[]{:S(2)}, u32[]{:S(2)}) collective-permute-start(s16[2,272,256]{2,1,0:T(8,128)(2,1)S(1)} %get-tuple-element.78), channel_id=1, source_target_pairs={{0,2},{1,3},{2,0},{3,1},{4,6},{5,7},{6,4},{7,5},{8,10},{9,11},{10,... | collective-permute-start | bytes 835592 | tf_op jit(solution)/shard_map/ppermute | solution.py:300
  106.3 15.0 %collective-permute-start.29 = (s16[2,272,256]{2,1,0:T(8,128)(2,1)S(1)}, s16[2,272,256]{2,1,0:T(8,128)(2,1)S(1)}, u32[]{:S(2)}, u32[]{:S(2)}) collective-permute-start(s16[2,272,256]{2,1,0:T(8,128)(2,1)S(1)} %get-tuple-element.85), channel_id=1, source_target_pairs={{0,2},{1,3},{2,0},{3,1},{4,6},{5,7},{6,4},{7,5},{8,10},{9,11},{10,... | collective-permute-start | bytes 835592 | tf_op jit(solution)/shard_map/ppermute | solution.py:300
  111.2 9.4 %collective-permute-start.28 = (s16[1,272,256]{2,1,0:T(8,128)(2,1)S(1)}, s16[1,272,256]{2,1,0:T(8,128)(2,1)S(1)}, u32[]{:S(2)}, u32[]{:S(2)}) collective-permute-start(s16[1,272,256]{2,1,0:T(8,128)(2,1)S(1)} %get-tuple-element.88), channel_id=1, source_target_pairs={{0,4},{1,5},{2,6},{3,7},{4,0},{5,1},{6,2},{7,3},{8,12},{9,13},{10,... | collective-permute-start | bytes 417800 | tf_op jit(solution)/shard_map/ppermute | solution.py:300
  125.9 9.4 %collective-permute-start.35 = (s16[272,256]{1,0:T(8,128)(2,1)S(1)}, s16[272,256]{1,0:T(8,128)(2,1)S(1)}, u32[]{:S(2)}, u32[]{:S(2)}) collective-permute-start(s16[272,256]{1,0:T(8,128)(2,1)S(1)} %finish.4.refs_0_), channel_id=1, source_target_pairs={{0,16},{8,24},{16,0},{24,8},{1,17},{9,25},{17,1},{25,9},{2,18},{10... | collective-permute-start | bytes 417800 | tf_op jit(solution)/shard_map/ppermute | solution.py:297
  (25 other events, 183.0 us)
where the time goes:
time: 141 us; the launch traced here: 142 us
  Pallas kernels  52.2 us (37%)
  starting transfers between devices  47.3 us (34%)
  waiting for transfers between devices  32.4 us (23%)
  other arithmetic  5.69 us (4%)
  local copies, waits for them, and re-layouts  3.99 us (3%)
    pallas_call x3, Pallas kernels, products(): pl.pallas_call(functools.partial(products_kernel, pieces), grid=(1,), in_...  36.3 us
    ppermute x29, starting transfers between devices, to_grp(): return lax.ppermute(v, 'grp', [(i, i ^ d) for i in range(4)])  36.2 us
    ppermute x29, waiting for transfers between devices, to_grp(): return lax.ppermute(v, 'grp', [(i, i ^ d) for i in range(4)])  20.8 us
    pallas_call x14, Pallas kernels, call(): pl.pallas_call(body, in_specs=in_smem(1) + in_vmem(len(args)), out_specs=...  11.1 us
    ppermute x6, starting transfers between devices, to_line(): return lax.ppermute(v, 'wide', [(i, i ^ 2 << b) for i in range(wide_count)])  10.4 us
    ppermute x6, waiting for transfers between devices, to_line(): return lax.ppermute(v, 'wide', [(i, i ^ 2 << b) for i in range(wide_count)])  7.96 us
    pallas_call x3, Pallas kernels, spread(): pl.pallas_call(spread_kernel, grid=(1,), in_specs=in_smem(1) + in_vmem(4)...  4.87 us
    ppermute x5, waiting for transfers between devices, to_core(): return lax.ppermute(v, 'wide', [(i, i ^ 1) for i in range(wide_count)])  3.65 us
  transfers between devices with their start and end apart: 40, of which 16 were waited for; matrix products, arithmetic and copies ran while one was open for 5% of the time, Pallas kernels for 35%

commit v1 on v0

--- a/solution.py
+++ b/solution.py
@@ -114,6 +114,12 @@
     return ref[pl.ds(0, side), :].astype(jnp.int32).astype(jnp.float32) * scale
 
 
+def hold_kernel(order_ref, tiles, out, sem):
+    copy = pltpu.make_async_copy(tiles, out, sem)
+    copy.start()
+    copy.wait()
+
+
 def join_kernel(order_ref, *refs):
     *parts, out = refs
     rows = parts[0].shape[0]
@@ -122,21 +128,12 @@
 
 
 def products_kernel(
-    pieces, ends_ref, source_ref, slot_ref, label_ref, own_tiles, sib_tiles, *refs
+    count_ref, source_ref, slot_ref, label_ref, own_tiles, sib_tiles, *refs
 ):
-    own_panel, near, far, *outs, held, stack, acc, sems = refs
-    tile_dev, side = held.shape[1], held.shape[2]
+    own_panel, near, far, *outs, stack, acc = refs
+    side = own_tiles.shape[1]
     shard = own_panel.shape[0] // side
     half = shard // 2
-    copies = []
-    for q, (which, first, count) in enumerate(pieces):
-        tiles = (own_tiles, sib_tiles)[which]
-        copies.append(
-            pltpu.make_async_copy(
-                tiles.at[pl.ds(first, count)], held.at[which, pl.ds(first, count)], sems.at[q]
-            )
-        )
-        copies[-1].start()
     for t in range(shard):
         stack[t] = own_panel[pl.ds(t * side, side), :]
     for i in range(3 * half):
@@ -148,31 +145,30 @@
     def _(i):
         acc[i] = jnp.zeros(acc.shape[1:], jnp.float32)
 
-    def some(which, at, count):
-        found = [
-            jnp.dot(
-                held[which, source_ref[which, at + u]],
-                stack[label_ref[which, at + u]],
-                preferred_element_type=jnp.float32,
-            )
-            for u in range(count)
-        ]
-        for u in range(count):
-            acc[slot_ref[which, at + u]] += found[u]
-
-    for q, (which, first, count) in enumerate(pieces):
-        copies[q].wait()
-        begin = 0 if first == 0 else ends_ref[q - 1]
-        end = ends_ref[q]
-        rounds = (end - begin) // UNROLL
+    for which, tiles in enumerate((own_tiles, sib_tiles)):
+
+        def some(at, count, which=which, tiles=tiles):
+            found = [
+                jnp.dot(
+                    tiles[source_ref[which, at + u]],
+                    stack[label_ref[which, at + u]],
+                    preferred_element_type=jnp.float32,
+                )
+                for u in range(count)
+            ]
+            for u in range(count):
+                acc[slot_ref[which, at + u]] += found[u]
+
+        count = count_ref[which]
+        rounds = count // UNROLL
 
         @pl.loop(0, rounds)
-        def _(i, which=which, begin=begin):
-            some(which, begin + i * UNROLL, UNROLL)
-
-        @pl.loop(begin + rounds * UNROLL, end)
-        def _(i, which=which):
-            some(which, i, 1)
+        def _(i, some=some):
+            some(i * UNROLL, UNROLL)
+
+        @pl.loop(rounds * UNROLL, count)
+        def _(i, some=some):
+            some(i, 1)
 
     sent = 0
     for out in outs:
@@ -332,14 +328,7 @@
     match = owner % 2 == core
     serial = jnp.broadcast_to(jnp.arange(tile_dev, dtype=jnp.int32), match.shape)
     source, in_plane, in_line, label = compact(match, [serial, in_plane, in_line, label])
-    cut = tile_dev // 4
-    pieces = ((0, 0, cut), (0, cut, tile_dev - cut), (1, 0, tile_dev))
-    ends = jnp.stack(
-        [
-            jnp.sum((match[which] & (serial[which] < first + count)).astype(jnp.int32))
-            for which, first, count in pieces
-        ]
-    )
+    found = jnp.sum(match.astype(jnp.int32), axis=-1)
 
     half, quarter = sums // 2, sums // 4
     coded = shape((side + CODE_ROWS, CHUNK), jnp.int16)
@@ -367,6 +356,18 @@
         last = done[0]
         return done
 
+    own_tiles = pl.pallas_call(
+        hold_kernel,
+        in_specs=in_smem(1) + in_any(1),
+        out_specs=in_vmem(1)[0],
+        out_shape=shape(tiles.shape, tiles.dtype),
+        scratch_shapes=[pltpu.SemaphoreType.DMA],
+        compiler_params=params(54),
+        cost_estimate=cost(0, 2 * tile_dev * side * side),
+        name="hold",
+    )(lax.optimization_barrier((bits, both))[0], tiles)
+    last = own_tiles
+
     def join(j):
         (joined,) = call(join_kernel, "join", [shape((3 * rows // 2, CHUNK), panel.dtype)], *near[j])
         return joined, to_core(joined)
@@ -374,24 +375,22 @@
     def products(j, slot, outs, joined, crossed):
         nonlocal last
         done = pl.pallas_call(
-            functools.partial(products_kernel, pieces),
+            products_kernel,
             grid=(1,),
             in_specs=in_smem(4)
-            + [pl.BlockSpec(memory_space=pltpu.HBM)] * 2
+            + in_vmem(2)
             + [pl.BlockSpec((rows, CHUNK), lambda i: (0, j))]
             + in_vmem(2),
             out_specs=in_vmem(len(outs)),
             out_shape=outs,
             scratch_shapes=[
-                pltpu.VMEM((2, tile_dev, side, side), tiles.dtype),
                 pltpu.VMEM((4 * shard, side, CHUNK), panel.dtype),
                 pltpu.VMEM((sums, side, CHUNK), jnp.float32),
-                pltpu.SemaphoreType.DMA((len(pieces),)),
             ],
-            compiler_params=params(54),
+            compiler_params=params(32),
             cost_estimate=cost(0, 4 * tile_dev * side * side),
             name="products",
-        )(in_order(ends), source, slot, label, tiles, sib_tiles, panel, joined, crossed)
+        )(in_order(found), source, slot, label, own_tiles, sib_tiles, panel, joined, crossed)
         last = done[0]
         return done
 

time: 141 us -> 132 us (0.936); the launches traced: 142 us -> 130 us
  Pallas kernels: 52.2 us -> 44.1 us
  other arithmetic: 5.69 us -> 2.02 us
  waiting for transfers between devices: 32.4 us -> 30.4 us
    pallas_call x3 -> x4, Pallas kernels: 36.3 us -> 28.2 us  [the longest x3 22 us: products(): pl.pallas_call(products_kernel, grid=(1,), in_specs=in_smem(4) + in_vmem(...]
    ppermute x5, waiting for transfers between devices: 3.65 us -> 0.12 us  [to_core(): return lax.ppermute(v, 'wide', [(i, i ^ 1) for i in range(wide_count)])]
    ppermute x29, waiting for transfers between devices: 20.8 us -> 23.6 us  [to_grp(): return lax.ppermute(v, 'grp', [(i, i ^ d) for i in range(4)])]
    another operation x1 -> x0, other arithmetic: 2.38 us -> none  [sums_plan(): jnp.stack([jnp.sum((match[which] & (serial[which] < first + count)).astyp...]
    ppermute x6, starting transfers between devices: 10.4 us -> 12.2 us  [to_line(): return lax.ppermute(v, 'wide', [(i, i ^ 2 << b) for i in range(wide_count)])]
  transfers between devices with their start and end apart: 40 -> 40, of which waited for: 16 -> 17; matrix products, arithmetic and copies ran while one was open for 5% -> 3% of each run, Pallas kernels for 35% -> 32%
where the time goes in v1:
time: 132 us; the launch traced here: 130 us
  starting transfers between devices  48.1 us (36%)
  Pallas kernels  44.1 us (33%)
  waiting for transfers between devices  30.4 us (23%)
  local copies, waits for them, and re-layouts  4.66 us (4%)
  other arithmetic  2.02 us (2%)
    ppermute x29, starting transfers between devices, to_grp(): return lax.ppermute(v, 'grp', [(i, i ^ d) for i in range(4)])  35.2 us
    ppermute x29, waiting for transfers between devices, to_grp(): return lax.ppermute(v, 'grp', [(i, i ^ d) for i in range(4)])  23.6 us
    pallas_call x3, Pallas kernels, products(): pl.pallas_call(products_kernel, grid=(1,), in_specs=in_smem(4) + in_vmem(...  22 us
    ppermute x6, starting transfers between devices, to_line(): return lax.ppermute(v, 'wide', [(i, i ^ 2 << b) for i in range(wide_count)])  12.2 us
    pallas_call x14, Pallas kernels, call(): pl.pallas_call(body, in_specs=in_smem(1) + in_vmem(len(args)), out_specs=...  11 us
    ppermute x6, waiting for transfers between devices, to_line(): return lax.ppermute(v, 'wide', [(i, i ^ 2 << b) for i in range(wide_count)])  6.72 us
    pallas_call x1, Pallas kernels, sums_plan(): pl.pallas_call(hold_kernel, in_specs=in_smem(1) + in_any(1), out_specs=in...  6.23 us
    pallas_call x3, Pallas kernels, spread(): pl.pallas_call(spread_kernel, grid=(1,), in_specs=in_smem(1) + in_vmem(4)...  4.87 us
  transfers between devices with their start and end apart: 40, of which 17 were waited for; matrix products, arithmetic and copies ran while one was open for 3% of the time, Pallas kernels for 32%

profile of v1, /device:TPU:0, one launch (start us, length us, event | category | flops | bytes accessed | tf_op | source)
XLA Modules:
  0.0 129.7 jit_solution(6447288633036079596)
XLA Ops:
  0.5 1.9 %constant_dynamic-slice_fusion.1 = (bf16[512,256]{1,0:T(8,128)(2,1)S(1)}, bf16[512,256]{1,0:T(8,128)(2,1)}, bf16[512,256]{1,0:T(8,128)(2,1)S(1)}) fusion(bf16[1024,768]{1,0:T(8,128)(2,1)} %refs_0_.5, s32[]{:T(128)S(6)} %select_n.204), kind=kLoop, calls=%fused_computation.68 | loop fusion | bytes 1572868 | tf_op jit(solution)/shard_map/dynamic_slice | solution.py:306
  2.3 3.4 %collective-permute-start.3 = (bf16[512,256]{1,0:T(8,128)(2,1)S(1)}, bf16[512,256]{1,0:T(8,128)(2,1)S(1)}, u32[]{:S(2)}, u32[]{:S(2)}) collective-permute-start(bf16[512,256]{1,0:T(8,128)(2,1)S(1)} %get-tuple-element.118), channel_id=1, source_target_pairs={{0,24},{8,16},{16,8},{24,0},{1,25},{9,17},{17,9},{25,1},{2,26},{10... | collective-permute-start | bytes 786440 | tf_op jit(solution)/shard_map/ppermute | solution.py:293
  7.7 6.2 %hold.1.own_tiles = bf16[48,256,256]{2,1,0:T(8,128)(2,1)} custom-call(s32[4]{0:T(128)} %pad_add_fusion.2.order_ref.bits_ref, bf16[48,256,256]{2,1,0:T(8,128)(2,1)} %tiles.1), custom_call_target="tpu_custom_call" | custom-call | bytes 6291456 | tf_op jit(solution)/shard_map/hold/pallas_call | solution.py:359
  14.1 4.3 %collective-permute-done.2.refs_1_ = bf16[512,256]{1,0:T(8,128)(2,1)S(1)} collective-permute-done((bf16[512,256]{1,0:T(8,128)(2,1)S(1)}, bf16[512,256]{1,0:T(8,128)(2,1)S(1)}, u32[]{:S(2)}, u32[]{:S(2)}) %collective-permute-start.2) | collective-permute-done | bytes 262176 | tf_op jit(solution)/shard_map/ppermute | solution.py:293
  23.5 2.8 %copy-done = bf16[48,256,256]{2,1,0:T(8,128)(2,1)S(1)} copy-done((bf16[48,256,256]{2,1,0:T(8,128)(2,1)S(1)}, bf16[48,256,256]{2,1,0:T(8,128)(2,1)}, u32[]{:S(2)}) %copy-start) | copy-done | bytes 6291480
  26.3 7.3 %products.3 = (s16[8,272,256]{2,1,0:T(8,128)(2,1)S(1)}, f32[8,256,256]{2,1,0:T(8,128)S(1)}) custom-call(s32[2]{0:T(128)S(1)} %convert_reduce_fusion.count_ref, s32[2,48]{1,0:T(2,128)S(1)} %get-tuple-element.110.source_ref, s32[2,48]{1,0:T(2,128)S(1)} %get-tuple-element.109.slot_ref, s32[2,48]{1,0:T(2,128)S(1)} %get-tuple-element.108.label_ref, ...), custom_call_target="tpu_custom_call" | custom-call | bytes 12582912 | tf_op jit(solution)/shard_map/products/pallas_call | solution.py:377
  40.9 7.3 %products.4 = (s16[4,272,256]{2,1,0:T(8,128)(2,1)S(1)}, s16[4,272,256]{2,1,0:T(8,128)(2,1)S(1)}, f32[8,256,256]{2,1,0:T(8,128)S(1)}) custom-call(s32[2]{0:T(128)S(1)} %convert_reduce_fusion.count_ref, s32[2,48]{1,0:T(2,128)S(1)} %get-tuple-element.110.source_ref, s32[2,48]{1,0:T(2,128)S(1)} %get-tuple-element.107.slot_ref, ...), custom_call_target="tpu_custom_call" | custom-call | bytes 12582912 | tf_op jit(solution)/shard_map/products/pallas_call | solution.py:377
  48.2 2.7 %collective-permute-done.11.refs_1_ = bf16[512,256]{1,0:T(8,128)(2,1)S(1)} collective-permute-done((bf16[512,256]{1,0:T(8,128)(2,1)S(1)}, bf16[512,256]{1,0:T(8,128)(2,1)S(1)}, u32[]{:S(2)}, u32[]{:S(2)}) %collective-permute-start.11) | collective-permute-done | bytes 262176 | tf_op jit(solution)/shard_map/ppermute | solution.py:293
  53.9 7.3 %products.5 = (s16[4,272,256]{2,1,0:T(8,128)(2,1)S(1)}, s16[4,272,256]{2,1,0:T(8,128)(2,1)S(1)}, f32[8,256,256]{2,1,0:T(8,128)S(1)}) custom-call(s32[2]{0:T(128)S(1)} %convert_reduce_fusion.count_ref, s32[2,48]{1,0:T(2,128)S(1)} %get-tuple-element.110.source_ref, s32[2,48]{1,0:T(2,128)S(1)} %get-tuple-element.107.slot_ref, ...), custom_call_target="tpu_custom_call" | custom-call | bytes 12582912 | tf_op jit(solution)/shard_map/products/pallas_call | solution.py:377
  61.3 2.9 %collective-permute-start.18 = (s16[4,272,256]{2,1,0:T(8,128)(2,1)S(1)}, s16[4,272,256]{2,1,0:T(8,128)(2,1)S(1)}, u32[]{:S(2)}, u32[]{:S(2)}) collective-permute-start(s16[4,272,256]{2,1,0:T(8,128)(2,1)S(1)} %get-tuple-element.76), channel_id=1, source_target_pairs={{0,16},{8,24},{16,0},{24,8},{1,17},{9,25},{17,1},{25,9},{2,18},{10... | collective-permute-start | bytes 1671176 | tf_op jit(solution)/shard_map/ppermute | solution.py:293
  66.5 2.7 %collective-permute-start.21 = (s16[4,272,256]{2,1,0:T(8,128)(2,1)S(1)}, s16[4,272,256]{2,1,0:T(8,128)(2,1)S(1)}, u32[]{:S(2)}, u32[]{:S(2)}) collective-permute-start(s16[4,272,256]{2,1,0:T(8,128)(2,1)S(1)} %get-tuple-element.70), channel_id=1, source_target_pairs={{0,4},{1,5},{2,6},{3,7},{4,0},{5,1},{6,2},{7,3},{8,12},{9,13},{10,... | collective-permute-start | bytes 1671176 | tf_op jit(solution)/shard_map/ppermute | solution.py:296
  70.3 1.8 %collective-permute-start.20 = (s16[2,272,256]{2,1,0:T(8,128)(2,1)S(1)}, s16[2,272,256]{2,1,0:T(8,128)(2,1)S(1)}, u32[]{:S(2)}, u32[]{:S(2)}) collective-permute-start(s16[2,272,256]{2,1,0:T(8,128)(2,1)S(1)} %get-tuple-element.80), channel_id=1, source_target_pairs={{0,8},{8,0},{16,24},{24,16},{1,9},{9,1},{17,25},{25,17},{2,10},{10... | collective-permute-start | bytes 835592 | tf_op jit(solution)/shard_map/ppermute | solution.py:293
  72.7 6.3 %collective-permute-done.18.recv_b = s16[4,272,256]{2,1,0:T(8,128)(2,1)S(1)} collective-permute-done((s16[4,272,256]{2,1,0:T(8,128)(2,1)S(1)}, s16[4,272,256]{2,1,0:T(8,128)(2,1)S(1)}, u32[]{:S(2)}, u32[]{:S(2)}) %collective-permute-start.18) | collective-permute-done | bytes 557088 | tf_op jit(solution)/shard_map/ppermute | solution.py:293
  83.9 2.7 %collective-permute-done.20.recv_b = s16[2,272,256]{2,1,0:T(8,128)(2,1)S(1)} collective-permute-done((s16[2,272,256]{2,1,0:T(8,128)(2,1)S(1)}, s16[2,272,256]{2,1,0:T(8,128)(2,1)S(1)}, u32[]{:S(2)}, u32[]{:S(2)}) %collective-permute-start.20) | collective-permute-done | bytes 278560 | tf_op jit(solution)/shard_map/ppermute | solution.py:293
  87.4 1.6 %collective-permute-start.24 = (s16[2,272,256]{2,1,0:T(8,128)(2,1)S(1)}, s16[2,272,256]{2,1,0:T(8,128)(2,1)S(1)}, u32[]{:S(2)}, u32[]{:S(2)}) collective-permute-start(s16[2,272,256]{2,1,0:T(8,128)(2,1)S(1)} %get-tuple-element.82), channel_id=1, source_target_pairs={{0,2},{1,3},{2,0},{3,1},{4,6},{5,7},{6,4},{7,5},{8,10},{9,11},{10,... | collective-permute-start | bytes 835592 | tf_op jit(solution)/shard_map/ppermute | solution.py:296
  89.0 4.2 %collective-permute-done.21.recv = s16[4,272,256]{2,1,0:T(8,128)(2,1)S(1)} collective-permute-done((s16[4,272,256]{2,1,0:T(8,128)(2,1)S(1)}, s16[4,272,256]{2,1,0:T(8,128)(2,1)S(1)}, u32[]{:S(2)}, u32[]{:S(2)}) %collective-permute-start.21) | collective-permute-done | bytes 557088 | tf_op jit(solution)/shard_map/ppermute | solution.py:296
  96.5 1.6 %collective-permute-start.27 = (s16[272,256]{1,0:T(8,128)(2,1)S(1)}, s16[272,256]{1,0:T(8,128)(2,1)S(1)}, u32[]{:S(2)}, u32[]{:S(2)}) collective-permute-start(s16[272,256]{1,0:T(8,128)(2,1)S(1)} %get-tuple-element.95), channel_id=1, source_target_pairs={{0,24},{8,16},{16,8},{24,0},{1,25},{9,17},{17,9},{25,1},{2,26},{10... | collective-permute-start | bytes 417800 | tf_op jit(solution)/shard_map/ppermute | solution.py:293
  99.8 3.1 %collective-permute-start.28 = (s16[1,272,256]{2,1,0:T(8,128)(2,1)S(1)}, s16[1,272,256]{2,1,0:T(8,128)(2,1)S(1)}, u32[]{:S(2)}, u32[]{:S(2)}) collective-permute-start(s16[1,272,256]{2,1,0:T(8,128)(2,1)S(1)} %get-tuple-element.92), channel_id=1, source_target_pairs={{0,4},{1,5},{2,6},{3,7},{4,0},{5,1},{6,2},{7,3},{8,12},{9,13},{10,... | collective-permute-start | bytes 417800 | tf_op jit(solution)/shard_map/ppermute | solution.py:296
  105.0 2.4 %collective-permute-start.32 = (s16[272,256]{1,0:T(8,128)(2,1)S(1)}, s16[272,256]{1,0:T(8,128)(2,1)S(1)}, u32[]{:S(2)}, u32[]{:S(2)}) collective-permute-start(s16[272,256]{1,0:T(8,128)(2,1)S(1)} %finish.3.refs_0_), channel_id=1, source_target_pairs={{0,24},{8,16},{16,8},{24,0},{1,25},{9,17},{17,9},{25,1},{2,26},{10... | collective-permute-start | bytes 417800 | tf_op jit(solution)/shard_map/ppermute | solution.py:293
  110.6 2.8 %collective-permute-start.33 = (s16[1,272,256]{2,1,0:T(8,128)(2,1)S(1)}, s16[1,272,256]{2,1,0:T(8,128)(2,1)S(1)}, u32[]{:S(2)}, u32[]{:S(2)}) collective-permute-start(s16[1,272,256]{2,1,0:T(8,128)(2,1)S(1)} %get-tuple-element.101), channel_id=1, source_target_pairs={{0,4},{1,5},{2,6},{3,7},{4,0},{5,1},{6,2},{7,3},{8,12},{9,13},{10,... | collective-permute-start | bytes 417800 | tf_op jit(solution)/shard_map/ppermute | solution.py:296
  113.4 2.3 %collective-permute-start.36 = (s16[272,256]{1,0:T(8,128)(2,1)S(1)}, s16[272,256]{1,0:T(8,128)(2,1)S(1)}, u32[]{:S(2)}, u32[]{:S(2)}) collective-permute-start(s16[272,256]{1,0:T(8,128)(2,1)S(1)} %finish.4.refs_0_), channel_id=1, source_target_pairs={{0,24},{8,16},{16,8},{24,0},{1,25},{9,17},{17,9},{25,1},{2,26},{10... | collective-permute-start | bytes 417800 | tf_op jit(solution)/shard_map/ppermute | solution.py:293
  123.5 1.6 %spread.4.refs_4_ = f32[1024,768]{1,0:T(8,128)} custom-call(s32[4]{0:T(128)S(1)} %copy-done.2, s16[272,256]{1,0:T(8,128)(2,1)S(1)} %finish.4.refs_0_, s16[272,256]{1,0:T(8,128)(2,1)S(1)} %collective-permute-done.34.refs_1_, s16[272,256]{1,0:T(8,128)(2,1)S(1)} %collective-permute-done.35.refs_2_, ...), custom_call_target="tpu_custom_call", output_to_operand_aliasing={{}: (5, {})} | custom-call | bytes 1572864 | tf_op jit(solution)/shard_map/spread/pallas_call | solution.py:401
  125.2 2.3 %collective-permute-done.39.refs_3_ = s16[272,256]{1,0:T(8,128)(2,1)S(1)} collective-permute-done((s16[272,256]{1,0:T(8,128)(2,1)S(1)}, s16[272,256]{1,0:T(8,128)(2,1)S(1)}, u32[]{:S(2)}, u32[]{:S(2)}) %collective-permute-start.39) | collective-permute-done | bytes 139296 | tf_op jit(solution)/shard_map/ppermute | solution.py:293
  128.1 1.6 %spread.5 = f32[1024,768]{1,0:T(8,128)} custom-call(s32[4]{0:T(128)S(1)} %copy-done.2, s16[272,256]{1,0:T(8,128)(2,1)S(1)} %finish.5.refs_0_, s16[272,256]{1,0:T(8,128)(2,1)S(1)} %collective-permute-done.37.refs_1_, s16[272,256]{1,0:T(8,128)(2,1)S(1)} %collective-permute-done.38.refs_2_, ...), custom_call_target="tpu_custom_call", output_to_operand_aliasing={{}: (5, {})} | custom-call | bytes 1572864 | tf_op jit(solution)/shard_map/spread/pallas_call | solution.py:401
  (96 shorter events, 46.1 us)
Async XLA Ops:
  0.0 23.5 %collective-permute-start.4 = (bf16[48,256,256]{2,1,0:T(8,128)(2,1)}, bf16[48,256,256]{2,1,0:T(8,128)(2,1)}, u32[]{:S(2)}, u32[]{:S(2)}) collective-permute-start(bf16[48,256,256]{2,1,0:T(8,128)(2,1)} %tiles.1), channel_id=1, source_target_pairs={{0,1},{1,0},{2,3},{3,2},{4,5},{5,4},{6,7},{7,6},{8,9},{9,8},{10,11... | collective-permute-start | bytes 18874376 | tf_op jit(solution)/shard_map/ppermute | solution.py:290
  2.3 11.8 %collective-permute-start.3 = (bf16[512,256]{1,0:T(8,128)(2,1)S(1)}, bf16[512,256]{1,0:T(8,128)(2,1)S(1)}, u32[]{:S(2)}, u32[]{:S(2)}) collective-permute-start(bf16[512,256]{1,0:T(8,128)(2,1)S(1)} %get-tuple-element.118), channel_id=1, source_target_pairs={{0,24},{8,16},{16,8},{24,0},{1,25},{9,17},{17,9},{25,1},{2,26},{10... | collective-permute-start | bytes 786440 | tf_op jit(solution)/shard_map/ppermute | solution.py:293
  5.8 12.6 %collective-permute-start.2 = (bf16[512,256]{1,0:T(8,128)(2,1)S(1)}, bf16[512,256]{1,0:T(8,128)(2,1)S(1)}, u32[]{:S(2)}, u32[]{:S(2)}) collective-permute-start(bf16[512,256]{1,0:T(8,128)(2,1)S(1)} %get-tuple-element.118), channel_id=1, source_target_pairs={{0,16},{8,24},{16,0},{24,8},{1,17},{9,25},{17,1},{25,9},{2,18},{10... | collective-permute-start | bytes 786440 | tf_op jit(solution)/shard_map/ppermute | solution.py:293
  6.3 12.4 %collective-permute-start.1 = (bf16[512,256]{1,0:T(8,128)(2,1)S(1)}, bf16[512,256]{1,0:T(8,128)(2,1)S(1)}, u32[]{:S(2)}, u32[]{:S(2)}) collective-permute-start(bf16[512,256]{1,0:T(8,128)(2,1)S(1)} %get-tuple-element.118), channel_id=1, source_target_pairs={{0,8},{8,0},{16,24},{24,16},{1,9},{9,1},{17,25},{25,17},{2,10},{10... | collective-permute-start | bytes 786440 | tf_op jit(solution)/shard_map/ppermute | solution.py:293
  19.6 14.0 %collective-permute-start.8 = (bf16[512,256]{1,0:T(8,128)(2,1)}, bf16[512,256]{1,0:T(8,128)(2,1)S(1)}, u32[]{:S(2)}, u32[]{:S(2)}) collective-permute-start(bf16[512,256]{1,0:T(8,128)(2,1)} %get-tuple-element.61), channel_id=1, source_target_pairs={{0,24},{8,16},{16,8},{24,0},{1,25},{9,17},{17,9},{25,1},{2,26},{10... | collective-permute-start | bytes 786440 | tf_op jit(solution)/shard_map/ppermute | solution.py:293
  21.1 14.0 %collective-permute-start.7 = (bf16[512,256]{1,0:T(8,128)(2,1)}, bf16[512,256]{1,0:T(8,128)(2,1)S(1)}, u32[]{:S(2)}, u32[]{:S(2)}) collective-permute-start(bf16[512,256]{1,0:T(8,128)(2,1)} %get-tuple-element.61), channel_id=1, source_target_pairs={{0,16},{8,24},{16,0},{24,8},{1,17},{9,25},{17,1},{25,9},{2,18},{10... | collective-permute-start | bytes 786440 | tf_op jit(solution)/shard_map/ppermute | solution.py:293
  22.6 12.5 %collective-permute-start.6 = (bf16[512,256]{1,0:T(8,128)(2,1)}, bf16[512,256]{1,0:T(8,128)(2,1)S(1)}, u32[]{:S(2)}, u32[]{:S(2)}) collective-permute-start(bf16[512,256]{1,0:T(8,128)(2,1)} %get-tuple-element.61), channel_id=1, source_target_pairs={{0,8},{8,0},{16,24},{24,16},{1,9},{9,1},{17,25},{25,17},{2,10},{10... | collective-permute-start | bytes 786440 | tf_op jit(solution)/shard_map/ppermute | solution.py:293
  35.8 12.5 %collective-permute-start.12 = (bf16[512,256]{1,0:T(8,128)(2,1)S(1)}, bf16[512,256]{1,0:T(8,128)(2,1)S(1)}, u32[]{:S(2)}, u32[]{:S(2)}) collective-permute-start(bf16[512,256]{1,0:T(8,128)(2,1)S(1)} %get-tuple-element.65), channel_id=1, source_target_pairs={{0,24},{8,16},{16,8},{24,0},{1,25},{9,17},{17,9},{25,1},{2,26},{10... | collective-permute-start | bytes 786440 | tf_op jit(solution)/shard_map/ppermute | solution.py:293
  37.3 13.6 %collective-permute-start.11 = (bf16[512,256]{1,0:T(8,128)(2,1)S(1)}, bf16[512,256]{1,0:T(8,128)(2,1)S(1)}, u32[]{:S(2)}, u32[]{:S(2)}) collective-permute-start(bf16[512,256]{1,0:T(8,128)(2,1)S(1)} %get-tuple-element.65), channel_id=1, source_target_pairs={{0,16},{8,24},{16,0},{24,8},{1,17},{9,25},{17,1},{25,9},{2,18},{10... | collective-permute-start | bytes 786440 | tf_op jit(solution)/shard_map/ppermute | solution.py:293
  38.7 12.2 %collective-permute-start.10 = (bf16[512,256]{1,0:T(8,128)(2,1)S(1)}, bf16[512,256]{1,0:T(8,128)(2,1)S(1)}, u32[]{:S(2)}, u32[]{:S(2)}) collective-permute-start(bf16[512,256]{1,0:T(8,128)(2,1)S(1)} %get-tuple-element.65), channel_id=1, source_target_pairs={{0,8},{8,0},{16,24},{24,16},{1,9},{9,1},{17,25},{25,17},{2,10},{10... | collective-permute-start | bytes 786440 | tf_op jit(solution)/shard_map/ppermute | solution.py:293
  39.3 26.1 %collective-permute-start.14 = (s16[8,272,256]{2,1,0:T(8,128)(2,1)S(1)}, s16[8,272,256]{2,1,0:T(8,128)(2,1)S(1)}, u32[]{:S(2)}, u32[]{:S(2)}) collective-permute-start(s16[8,272,256]{2,1,0:T(8,128)(2,1)S(1)} %get-tuple-element.59), channel_id=1, source_target_pairs={{0,2},{1,3},{2,0},{3,1},{4,6},{5,7},{6,4},{7,5},{8,10},{9,11},{10,... | collective-permute-start | bytes 3342344 | tf_op jit(solution)/shard_map/ppermute | solution.py:296
  51.7 17.5 %collective-permute-start.16 = (s16[4,272,256]{2,1,0:T(8,128)(2,1)S(1)}, s16[4,272,256]{2,1,0:T(8,128)(2,1)S(1)}, u32[]{:S(2)}, u32[]{:S(2)}) collective-permute-start(s16[4,272,256]{2,1,0:T(8,128)(2,1)S(1)} %get-tuple-element.72), channel_id=1, source_target_pairs={{0,16},{8,24},{16,0},{24,8},{1,17},{9,25},{17,1},{25,9},{2,18},{10... | collective-permute-start | bytes 1671176 | tf_op jit(solution)/shard_map/ppermute | solution.py:293
  53.1 16.0 %collective-permute-start.15 = (s16[4,272,256]{2,1,0:T(8,128)(2,1)S(1)}, s16[4,272,256]{2,1,0:T(8,128)(2,1)S(1)}, u32[]{:S(2)}, u32[]{:S(2)}) collective-permute-start(s16[4,272,256]{2,1,0:T(8,128)(2,1)S(1)} %get-tuple-element.63), channel_id=1, source_target_pairs={{0,8},{8,0},{16,24},{24,16},{1,9},{9,1},{17,25},{25,17},{2,10},{10... | collective-permute-start | bytes 1671176 | tf_op jit(solution)/shard_map/ppermute | solution.py:293
  61.3 17.8 %collective-permute-start.18 = (s16[4,272,256]{2,1,0:T(8,128)(2,1)S(1)}, s16[4,272,256]{2,1,0:T(8,128)(2,1)S(1)}, u32[]{:S(2)}, u32[]{:S(2)}) collective-permute-start(s16[4,272,256]{2,1,0:T(8,128)(2,1)S(1)} %get-tuple-element.76), channel_id=1, source_target_pairs={{0,16},{8,24},{16,0},{24,8},{1,17},{9,25},{17,1},{25,9},{2,18},{10... | collective-permute-start | bytes 1671176 | tf_op jit(solution)/shard_map/ppermute | solution.py:293
  64.1 16.4 %collective-permute-start.17 = (s16[4,272,256]{2,1,0:T(8,128)(2,1)S(1)}, s16[4,272,256]{2,1,0:T(8,128)(2,1)S(1)}, u32[]{:S(2)}, u32[]{:S(2)}) collective-permute-start(s16[4,272,256]{2,1,0:T(8,128)(2,1)S(1)} %get-tuple-element.67), channel_id=1, source_target_pairs={{0,8},{8,0},{16,24},{24,16},{1,9},{9,1},{17,25},{25,17},{2,10},{10... | collective-permute-start | bytes 1671176 | tf_op jit(solution)/shard_map/ppermute | solution.py:293
  66.5 26.7 %collective-permute-start.21 = (s16[4,272,256]{2,1,0:T(8,128)(2,1)S(1)}, s16[4,272,256]{2,1,0:T(8,128)(2,1)S(1)}, u32[]{:S(2)}, u32[]{:S(2)}) collective-permute-start(s16[4,272,256]{2,1,0:T(8,128)(2,1)S(1)} %get-tuple-element.70), channel_id=1, source_target_pairs={{0,4},{1,5},{2,6},{3,7},{4,0},{5,1},{6,2},{7,3},{8,12},{9,13},{10,... | collective-permute-start | bytes 1671176 | tf_op jit(solution)/shard_map/ppermute | solution.py:296
  70.3 16.2 %collective-permute-start.20 = (s16[2,272,256]{2,1,0:T(8,128)(2,1)S(1)}, s16[2,272,256]{2,1,0:T(8,128)(2,1)S(1)}, u32[]{:S(2)}, u32[]{:S(2)}) collective-permute-start(s16[2,272,256]{2,1,0:T(8,128)(2,1)S(1)} %get-tuple-element.80), channel_id=1, source_target_pairs={{0,8},{8,0},{16,24},{24,16},{1,9},{9,1},{17,25},{25,17},{2,10},{10... | collective-permute-start | bytes 835592 | tf_op jit(solution)/shard_map/ppermute | solution.py:293
  72.1 14.4 %collective-permute-start.19 = (s16[2,272,256]{2,1,0:T(8,128)(2,1)S(1)}, s16[2,272,256]{2,1,0:T(8,128)(2,1)S(1)}, u32[]{:S(2)}, u32[]{:S(2)}) collective-permute-start(s16[2,272,256]{2,1,0:T(8,128)(2,1)S(1)} %get-tuple-element.74), channel_id=1, source_target_pairs={{0,16},{8,24},{16,0},{24,8},{1,17},{9,25},{17,1},{25,9},{2,18},{10... | collective-permute-start | bytes 835592 | tf_op jit(solution)/shard_map/ppermute | solution.py:293
  81.7 12.3 %collective-permute-start.23 = (s16[2,272,256]{2,1,0:T(8,128)(2,1)S(1)}, s16[2,272,256]{2,1,0:T(8,128)(2,1)S(1)}, u32[]{:S(2)}, u32[]{:S(2)}) collective-permute-start(s16[2,272,256]{2,1,0:T(8,128)(2,1)S(1)} %get-tuple-element.87), channel_id=1, source_target_pairs={{0,8},{8,0},{16,24},{24,16},{1,9},{9,1},{17,25},{25,17},{2,10},{10... | collective-permute-start | bytes 835592 | tf_op jit(solution)/shard_map/ppermute | solution.py:293
  82.4 11.6 %collective-permute-start.22 = (s16[2,272,256]{2,1,0:T(8,128)(2,1)S(1)}, s16[2,272,256]{2,1,0:T(8,128)(2,1)S(1)}, u32[]{:S(2)}, u32[]{:S(2)}) collective-permute-start(s16[2,272,256]{2,1,0:T(8,128)(2,1)S(1)} %get-tuple-element.78), channel_id=1, source_target_pairs={{0,16},{8,24},{16,0},{24,8},{1,17},{9,25},{17,1},{25,9},{2,18},{10... | collective-permute-start | bytes 835592 | tf_op jit(solution)/shard_map/ppermute | solution.py:293
  87.4 11.8 %collective-permute-start.24 = (s16[2,272,256]{2,1,0:T(8,128)(2,1)S(1)}, s16[2,272,256]{2,1,0:T(8,128)(2,1)S(1)}, u32[]{:S(2)}, u32[]{:S(2)}) collective-permute-start(s16[2,272,256]{2,1,0:T(8,128)(2,1)S(1)} %get-tuple-element.82), channel_id=1, source_target_pairs={{0,2},{1,3},{2,0},{3,1},{4,6},{5,7},{6,4},{7,5},{8,10},{9,11},{10,... | collective-permute-start | bytes 835592 | tf_op jit(solution)/shard_map/ppermute | solution.py:296
  94.9 15.0 %collective-permute-start.29 = (s16[2,272,256]{2,1,0:T(8,128)(2,1)S(1)}, s16[2,272,256]{2,1,0:T(8,128)(2,1)S(1)}, u32[]{:S(2)}, u32[]{:S(2)}) collective-permute-start(s16[2,272,256]{2,1,0:T(8,128)(2,1)S(1)} %get-tuple-element.89), channel_id=1, source_target_pairs={{0,2},{1,3},{2,0},{3,1},{4,6},{5,7},{6,4},{7,5},{8,10},{9,11},{10,... | collective-permute-start | bytes 835592 | tf_op jit(solution)/shard_map/ppermute | solution.py:296
  99.8 9.4 %collective-permute-start.28 = (s16[1,272,256]{2,1,0:T(8,128)(2,1)S(1)}, s16[1,272,256]{2,1,0:T(8,128)(2,1)S(1)}, u32[]{:S(2)}, u32[]{:S(2)}) collective-permute-start(s16[1,272,256]{2,1,0:T(8,128)(2,1)S(1)} %get-tuple-element.92), channel_id=1, source_target_pairs={{0,4},{1,5},{2,6},{3,7},{4,0},{5,1},{6,2},{7,3},{8,12},{9,13},{10,... | collective-permute-start | bytes 417800 | tf_op jit(solution)/shard_map/ppermute | solution.py:296
  105.0 10.7 %collective-permute-start.32 = (s16[272,256]{1,0:T(8,128)(2,1)S(1)}, s16[272,256]{1,0:T(8,128)(2,1)S(1)}, u32[]{:S(2)}, u32[]{:S(2)}) collective-permute-start(s16[272,256]{1,0:T(8,128)(2,1)S(1)} %finish.3.refs_0_), channel_id=1, source_target_pairs={{0,24},{8,16},{16,8},{24,0},{1,25},{9,17},{17,9},{25,1},{2,26},{10... | collective-permute-start | bytes 417800 | tf_op jit(solution)/shard_map/ppermute | solution.py:293
  (20 other events, 139.6 us)

commit v2 on v1

--- a/solution.py
+++ b/solution.py
@@ -13,7 +13,7 @@
 CODE_STEPS = 256.0
 TOP = 32000.0
 CHUNK = 256
-UNROLL = 4
+UNROLL = 8
 LOG2 = math.log(2.0)
 
 
@@ -128,18 +128,15 @@
 
 
 def products_kernel(
-    count_ref, source_ref, slot_ref, label_ref, own_tiles, sib_tiles, *refs
+    fill, rounds_ref, source_ref, slot_ref, label_ref, own_tiles, sib_tiles, own_panel, *refs
 ):
-    own_panel, near, far, *outs, stack, acc = refs
+    parts = refs[: 1 + max(which for which, _, _ in fill)]
+    *outs, stack, acc = refs[len(parts) :]
     side = own_tiles.shape[1]
-    shard = own_panel.shape[0] // side
-    half = shard // 2
-    for t in range(shard):
+    for t in range(own_panel.shape[0] // side):
         stack[t] = own_panel[pl.ds(t * side, side), :]
-    for i in range(3 * half):
-        at = shard + (i // half) * shard + i % half
-        stack[at] = near[pl.ds(i * side, side), :]
-        stack[at + half] = far[pl.ds(i * side, side), :]
+    for which, t, at in fill:
+        stack[at] = parts[which][pl.ds(t * side, side), :]
 
     @pl.loop(0, acc.shape[0])
     def _(i):
@@ -147,28 +144,18 @@
 
     for which, tiles in enumerate((own_tiles, sib_tiles)):
 
-        def some(at, count, which=which, tiles=tiles):
+        @pl.loop(0, rounds_ref[which])
+        def _(i, which=which, tiles=tiles):
             found = [
                 jnp.dot(
-                    tiles[source_ref[which, at + u]],
-                    stack[label_ref[which, at + u]],
+                    tiles[source_ref[which, i * UNROLL + u]],
+                    stack[label_ref[which, i * UNROLL + u]],
                     preferred_element_type=jnp.float32,
                 )
-                for u in range(count)
+                for u in range(UNROLL)
             ]
-            for u in range(count):
-                acc[slot_ref[which, at + u]] += found[u]
-
-        count = count_ref[which]
-        rounds = count // UNROLL
-
-        @pl.loop(0, rounds)
-        def _(i, some=some):
-            some(i * UNROLL, UNROLL)
-
-        @pl.loop(rounds * UNROLL, count)
-        def _(i, some=some):
-            some(i, 1)
+            for u in range(UNROLL):
+                acc[slot_ref[which, i * UNROLL + u]] += found[u]
 
     sent = 0
     for out in outs:
@@ -268,7 +255,7 @@
 
 
 def compact(match, values):
-    count = match.shape[-1]
+    count = -(-match.shape[-1] // UNROLL) * UNROLL
     rank = jnp.cumsum(match.astype(jnp.int32), axis=-1) - 1
     at = jnp.arange(count, dtype=jnp.int32)
     hit = match[:, None, :] & (rank[:, None, :] == at[None, :, None])
@@ -302,14 +289,15 @@
     both = jnp.stack([labels, to_core(labels)])
     sib_tiles = to_core(tiles)
 
-    mines = [
-        lax.dynamic_slice(panel, (core * (rows // 2), j * CHUNK), (rows // 2, CHUNK))
-        for j in range(chunks)
-    ]
-    near = [[to_grp(mines[0], d) for d in (1, 2, 3)]]
-    for mine in mines[1:]:
-        mine = lax.optimization_barrier((mine, *near[-1]))[0]
-        near.append([to_grp(mine, d) for d in (1, 2, 3)])
+    def own_half(source, j):
+        return lax.dynamic_slice(source, (core * (rows // 2), j * CHUNK), (rows // 2, CHUNK))
+
+    mine = own_half(panel, 0)
+    near = [to_grp(mine, d) for d in (1, 2, 3)]
+    later = lax.optimization_barrier((panel, *near))[0]
+    ways = [None, (1, 2), (2, 1)]
+    mines = [mine] + [own_half(later, j) for j in range(1, chunks)]
+    firsts = [None] + [to_grp(mines[j], ways[j][0]) for j in range(1, chunks)]
 
     table_ids = jnp.arange(owner_map.shape[0], dtype=jnp.int32)
     position = jnp.sum(jnp.where(both[:, 0, :, None] == table_ids, owner_map, 0), axis=-1)
@@ -329,6 +317,10 @@
     serial = jnp.broadcast_to(jnp.arange(tile_dev, dtype=jnp.int32), match.shape)
     source, in_plane, in_line, label = compact(match, [serial, in_plane, in_line, label])
     found = jnp.sum(match.astype(jnp.int32), axis=-1)
+    rounds = (found + UNROLL - 1) // UNROLL
+    beyond = jnp.arange(source.shape[-1], dtype=jnp.int32) >= found[:, None]
+    in_plane = jnp.where(beyond, sums, in_plane)
+    in_line = jnp.where(beyond, sums, in_line)
 
     half, quarter = sums // 2, sums // 4
     coded = shape((side + CODE_ROWS, CHUNK), jnp.int16)
@@ -362,35 +354,61 @@
         out_specs=in_vmem(1)[0],
         out_shape=shape(tiles.shape, tiles.dtype),
         scratch_shapes=[pltpu.SemaphoreType.DMA],
-        compiler_params=params(54),
+        compiler_params=params(16),
         cost_estimate=cost(0, 2 * tile_dev * side * side),
         name="hold",
     )(lax.optimization_barrier((bits, both))[0], tiles)
     last = own_tiles
 
+    def places(operand, tiles_of, first):
+        return [
+            (operand, t, d * shard + first + i % part)
+            for i, (t, d) in enumerate((t, d) for d, ts in tiles_of for t in ts)
+        ]
+
+    part = shard // 2
+
     def join(j):
-        (joined,) = call(join_kernel, "join", [shape((3 * rows // 2, CHUNK), panel.dtype)], *near[j])
-        return joined, to_core(joined)
-
-    def products(j, slot, outs, joined, crossed):
+        (joined,) = call(join_kernel, "join", [shape((3 * rows // 2, CHUNK), panel.dtype)], *near)
+        tiles_of = [(d, range((d - 1) * part, d * part)) for d in (1, 2, 3)]
+        fill = places(0, tiles_of, 0) + places(1, tiles_of, part)
+        return fill, [joined, to_core(joined)]
+
+    def pair(j):
+        way, other = ways[j]
+        (joined,) = call(
+            join_kernel, "join", [shape((rows, CHUNK), panel.dtype)], mines[j], firsts[j]
+        )
+        second = to_grp(joined, other)
+        in_first = [(way, range(part, 2 * part))]
+        in_second = [(other, range(part)), (way ^ other, range(part, 2 * part))]
+        fill = (
+            places(0, in_first, 0)
+            + places(1, in_first, part)
+            + places(2, in_second, 0)
+            + places(3, in_second, part)
+        )
+        return fill, [joined, to_core(joined), second, to_core(second)]
+
+    def products(j, slot, outs, fill, parts):
         nonlocal last
         done = pl.pallas_call(
-            products_kernel,
+            functools.partial(products_kernel, tuple(fill)),
             grid=(1,),
             in_specs=in_smem(4)
             + in_vmem(2)
             + [pl.BlockSpec((rows, CHUNK), lambda i: (0, j))]
-            + in_vmem(2),
+            + in_vmem(len(parts)),
             out_specs=in_vmem(len(outs)),
             out_shape=outs,
             scratch_shapes=[
                 pltpu.VMEM((4 * shard, side, CHUNK), panel.dtype),
-                pltpu.VMEM((sums, side, CHUNK), jnp.float32),
+                pltpu.VMEM((sums + 1, side, CHUNK), jnp.float32),
             ],
             compiler_params=params(32),
             cost_estimate=cost(0, 4 * tile_dev * side * side),
             name="products",
-        )(in_order(found), source, slot, label, own_tiles, sib_tiles, panel, joined, crossed)
+        )(in_order(rounds), source, slot, label, own_tiles, sib_tiles, panel, *parts)
         last = done[0]
         return done
 
@@ -412,10 +430,10 @@
         return last
 
     def line_first(j):
-        joined, crossed = join(j)
+        panel_of = join(j)
         yield
         send, keep = products(
-            j, in_line, [stack_of(half, coded), stack_of(half, plain)], joined, crossed
+            j, in_line, [stack_of(half, coded), stack_of(half, plain)], *panel_of
         )
         yield
         recv = to_line(send, 0)
@@ -431,10 +449,10 @@
         yield done
 
     def plane_first(j):
-        joined, crossed = join(j)
+        panel_of = pair(j)
         yield
         send_a, send_b, keep = products(
-            j, in_plane, [stack_of(quarter, coded)] * 2 + [stack_of(half, plain)], joined, crossed
+            j, in_plane, [stack_of(quarter, coded)] * 2 + [stack_of(half, plain)], *panel_of
         )
         yield
         send_a, send_b, keep = call(
@@ -471,7 +489,7 @@
     steps, lengths = [0] * chunks, [5] + [6] * (chunks - 1)
     work = [(line_first if j == 0 else plane_first)(j) for j in range(chunks)]
     dones, result = {}, None
-    for j in (0, 0, 1, 1, 2, 2, 0, 1, 2, 1, 0, 2, 1, 0, 1, 2, 0, 2, 1, 2):
+    for j in (0, 0, 1, 2, 1, 2, 0, 1, 2, 1, 0, 2, 1, 0, 1, 2, 0, 2, 1, 2):
         if j in dones:
             result = spread(j, dones[j], result)
             continue

time: 132 us -> 132 us (level)
  waiting for transfers between devices: 30.4 us -> 36.4 us
  starting transfers between devices: 48.1 us -> 42.6 us
  local copies, waits for them, and re-layouts: 4.66 us -> 9.23 us
  Pallas kernels: 44.1 us -> 39.9 us
    ppermute x29 -> x27, waiting for transfers between devices: 23.6 us -> 33.7 us  [to_grp(): return lax.ppermute(v, 'grp', [(i, i ^ d) for i in range(4)])]
    unnamed x8 -> x10, local copies, waits for them, and re-layouts: 2.79 us -> 8.22 us
    pallas_call x1, Pallas kernels: 6.23 us -> 0.97 us  [sums_plan(): pl.pallas_call(hold_kernel, in_specs=in_smem(1) + in_any(1), out_specs=in...]
    ppermute x6, waiting for transfers between devices: 6.72 us -> 2.55 us  [to_line(): return lax.ppermute(v, 'wide', [(i, i ^ 2 << b) for i in range(wide_count)])]
    ppermute x6, starting transfers between devices: 12.2 us -> 9.04 us  [to_line(): return lax.ppermute(v, 'wide', [(i, i ^ 2 << b) for i in range(wide_count)])]
    ppermute x29 -> x27, starting transfers between devices: 35.2 us -> 32.4 us  [to_grp(): return lax.ppermute(v, 'grp', [(i, i ^ d) for i in range(4)])]
  transfers between devices with their start and end apart: 40 -> 40, of which waited for: 17 -> 17; matrix products, arithmetic and copies ran while one was open for 3% -> 2% of each run, Pallas kernels for 32% -> 29%
where the time goes in v2:
time: 132 us; the launch traced here: 130 us
  starting transfers between devices  42.6 us (32%)
  Pallas kernels  39.9 us (30%)
  waiting for transfers between devices  36.4 us (28%)
  local copies, waits for them, and re-layouts  9.23 us (7%)
  other arithmetic  1.59 us (1%)
    ppermute x27, waiting for transfers between devices, to_grp(): return lax.ppermute(v, 'grp', [(i, i ^ d) for i in range(4)])  33.7 us
    ppermute x27, starting transfers between devices, to_grp(): return lax.ppermute(v, 'grp', [(i, i ^ d) for i in range(4)])  32.4 us
    pallas_call x3, Pallas kernels, products(): pl.pallas_call(functools.partial(products_kernel, tuple(fill)), grid=(1,)...  23.1 us
    pallas_call x14, Pallas kernels, call(): pl.pallas_call(body, in_specs=in_smem(1) + in_vmem(len(args)), out_specs=...  11 us
    ppermute x6, starting transfers between devices, to_line(): return lax.ppermute(v, 'wide', [(i, i ^ 2 << b) for i in range(wide_count)])  9.04 us
    unnamed x10, local copies, waits for them, and re-layouts  8.22 us
    pallas_call x3, Pallas kernels, spread(): pl.pallas_call(spread_kernel, grid=(1,), in_specs=in_smem(1) + in_vmem(4)...  4.87 us
  transfers between devices with their start and end apart: 40, of which 17 were waited for; matrix products, arithmetic and copies ran while one was open for 2% of the time, Pallas kernels for 29%

profile of v2, /device:TPU:0, one launch (start us, length us, event | category | flops | bytes accessed | tf_op | source)
XLA Modules:
  0.0 130.1 jit_solution(13180813683738714560)
XLA Ops:
  1.4 3.5 %collective-permute-start.3 = (bf16[512,256]{1,0:T(8,128)(2,1)S(1)}, bf16[512,256]{1,0:T(8,128)(2,1)S(1)}, u32[]{:S(2)}, u32[]{:S(2)}) collective-permute-start(bf16[512,256]{1,0:T(8,128)(2,1)S(1)} %constant_dynamic-slice_fusion.2), channel_id=1, source_target_pairs={{0,24},{8,16},{16,8},{24,0},{1,25},{9,17},{17,9},{25,1},{2,26},{10... | collective-permute-start | bytes 786440 | tf_op jit(solution)/shard_map/ppermute | solution.py:280
  6.4 2.8 %copy-done.3 = bf16[48,256,256]{2,1,0:T(8,128)(2,1)S(1)} copy-done((bf16[48,256,256]{2,1,0:T(8,128)(2,1)S(1)}, bf16[48,256,256]{2,1,0:T(8,128)(2,1)}, u32[]{:S(2)}) %copy-start.3) | copy-done | bytes 6291480
  10.2 2.6 %copy-done = bf16[48,256,256]{2,1,0:T(8,128)(2,1)} copy-done((bf16[48,256,256]{2,1,0:T(8,128)(2,1)}, bf16[48,256,256]{2,1,0:T(8,128)(2,1)S(1)}, u32[]{:S(2)}) %copy-start) | copy-done | bytes 6291480
  13.3 4.3 %collective-permute-done.2.refs_1_ = bf16[512,256]{1,0:T(8,128)(2,1)S(1)} collective-permute-done((bf16[512,256]{1,0:T(8,128)(2,1)S(1)}, bf16[512,256]{1,0:T(8,128)(2,1)S(1)}, u32[]{:S(2)}, u32[]{:S(2)}) %collective-permute-start.2) | collective-permute-done | bytes 262176 | tf_op jit(solution)/shard_map/ppermute | solution.py:280
  18.9 1.6 %collective-permute-start.6 = (bf16[512,256]{1,0:T(8,128)(2,1)S(1)}, bf16[512,256]{1,0:T(8,128)(2,1)S(1)}, u32[]{:S(2)}, u32[]{:S(2)}) collective-permute-start(bf16[512,256]{1,0:T(8,128)(2,1)S(1)} %get-tuple-element.115.refs_0_), channel_id=1, source_target_pairs={{0,8},{8,0},{16,24},{24,16},{1,9},{9,1},{17,25},{25,17},{2,10},{10... | collective-permute-start | bytes 786440 | tf_op jit(solution)/shard_map/ppermute | solution.py:280
  21.2 2.8 %copy-done.1 = bf16[48,256,256]{2,1,0:T(8,128)(2,1)S(1)} copy-done((bf16[48,256,256]{2,1,0:T(8,128)(2,1)S(1)}, bf16[48,256,256]{2,1,0:T(8,128)(2,1)}, u32[]{:S(2)}) %copy-start.1) | copy-done | bytes 6291480
  24.0 7.7 %products.3 = (s16[8,272,256]{2,1,0:T(8,128)(2,1)S(1)}, f32[8,256,256]{2,1,0:T(8,128)S(1)}) custom-call(s32[2]{0:T(128)S(1)} %and_select_fusion.10.rounds_ref, s32[2,48]{1,0:T(2,128)S(1)} %get-tuple-element.108.source_ref, s32[2,48]{1,0:T(2,128)S(1)} %get-tuple-element.121.slot_ref, s32[2,48]{1,0:T(2,128)S(1)} %get-tuple-element.106.label_ref, ...), custom_call_target="tpu_custom_call" | custom-call | bytes 12582912 | tf_op jit(solution)/shard_map/products/pallas_call | solution.py:395
  35.7 9.4 %collective-permute-done.9.refs_2_ = bf16[1024,256]{1,0:T(8,128)(2,1)S(1)} collective-permute-done((bf16[1024,256]{1,0:T(8,128)(2,1)S(1)}, bf16[1024,256]{1,0:T(8,128)(2,1)S(1)}, u32[]{:S(2)}, u32[]{:S(2)}) %collective-permute-start.9) | collective-permute-done | bytes 524320 | tf_op jit(solution)/shard_map/ppermute | solution.py:280
  47.0 7.7 %products.4 = (s16[4,272,256]{2,1,0:T(8,128)(2,1)S(1)}, s16[4,272,256]{2,1,0:T(8,128)(2,1)S(1)}, f32[8,256,256]{2,1,0:T(8,128)S(1)}) custom-call(s32[2]{0:T(128)S(1)} %and_select_fusion.10.rounds_ref, s32[2,48]{1,0:T(2,128)S(1)} %get-tuple-element.108.source_ref, s32[2,48]{1,0:T(2,128)S(1)} %get-tuple-element.120.slot_ref, ...), custom_call_target="tpu_custom_call" | custom-call | bytes 12582912 | tf_op jit(solution)/shard_map/products/pallas_call | solution.py:395
  56.8 7.7 %products.5 = (s16[4,272,256]{2,1,0:T(8,128)(2,1)S(1)}, s16[4,272,256]{2,1,0:T(8,128)(2,1)S(1)}, f32[8,256,256]{2,1,0:T(8,128)S(1)}) custom-call(s32[2]{0:T(128)S(1)} %and_select_fusion.10.rounds_ref, s32[2,48]{1,0:T(2,128)S(1)} %get-tuple-element.108.source_ref, s32[2,48]{1,0:T(2,128)S(1)} %get-tuple-element.120.slot_ref, ...), custom_call_target="tpu_custom_call" | custom-call | bytes 12582912 | tf_op jit(solution)/shard_map/products/pallas_call | solution.py:395
  68.2 1.7 %collective-permute-start.21 = (s16[4,272,256]{2,1,0:T(8,128)(2,1)S(1)}, s16[4,272,256]{2,1,0:T(8,128)(2,1)S(1)}, u32[]{:S(2)}, u32[]{:S(2)}) collective-permute-start(s16[4,272,256]{2,1,0:T(8,128)(2,1)S(1)} %get-tuple-element.68), channel_id=1, source_target_pairs={{0,4},{1,5},{2,6},{3,7},{4,0},{5,1},{6,2},{7,3},{8,12},{9,13},{10,... | collective-permute-start | bytes 1671176 | tf_op jit(solution)/shard_map/ppermute | solution.py:283
  75.0 7.3 %collective-permute-done.18.recv_b = s16[4,272,256]{2,1,0:T(8,128)(2,1)S(1)} collective-permute-done((s16[4,272,256]{2,1,0:T(8,128)(2,1)S(1)}, s16[4,272,256]{2,1,0:T(8,128)(2,1)S(1)}, u32[]{:S(2)}, u32[]{:S(2)}) %collective-permute-start.18) | collective-permute-done | bytes 557088 | tf_op jit(solution)/shard_map/ppermute | solution.py:280
  86.9 2.8 %collective-permute-done.20.recv_b = s16[2,272,256]{2,1,0:T(8,128)(2,1)S(1)} collective-permute-done((s16[2,272,256]{2,1,0:T(8,128)(2,1)S(1)}, s16[2,272,256]{2,1,0:T(8,128)(2,1)S(1)}, u32[]{:S(2)}, u32[]{:S(2)}) %collective-permute-start.20) | collective-permute-done | bytes 278560 | tf_op jit(solution)/shard_map/ppermute | solution.py:280
  91.3 2.5 %collective-permute-done.21.recv = s16[4,272,256]{2,1,0:T(8,128)(2,1)S(1)} collective-permute-done((s16[4,272,256]{2,1,0:T(8,128)(2,1)S(1)}, s16[4,272,256]{2,1,0:T(8,128)(2,1)S(1)}, u32[]{:S(2)}, u32[]{:S(2)}) %collective-permute-start.21) | collective-permute-done | bytes 557088 | tf_op jit(solution)/shard_map/ppermute | solution.py:283
  97.0 1.7 %collective-permute-start.26 = (s16[272,256]{1,0:T(8,128)(2,1)S(1)}, s16[272,256]{1,0:T(8,128)(2,1)S(1)}, u32[]{:S(2)}, u32[]{:S(2)}) collective-permute-start(s16[272,256]{1,0:T(8,128)(2,1)S(1)} %get-tuple-element.92), channel_id=1, source_target_pairs={{0,16},{8,24},{16,0},{24,8},{1,17},{9,25},{17,1},{25,9},{2,18},{10... | collective-permute-start | bytes 417800 | tf_op jit(solution)/shard_map/ppermute | solution.py:280
  101.2 2.7 %collective-permute-start.28 = (s16[1,272,256]{2,1,0:T(8,128)(2,1)S(1)}, s16[1,272,256]{2,1,0:T(8,128)(2,1)S(1)}, u32[]{:S(2)}, u32[]{:S(2)}) collective-permute-start(s16[1,272,256]{2,1,0:T(8,128)(2,1)S(1)} %get-tuple-element.90), channel_id=1, source_target_pairs={{0,4},{1,5},{2,6},{3,7},{4,0},{5,1},{6,2},{7,3},{8,12},{9,13},{10,... | collective-permute-start | bytes 417800 | tf_op jit(solution)/shard_map/ppermute | solution.py:283
  104.4 1.6 %collective-permute-done.27.refs_2_ = s16[272,256]{1,0:T(8,128)(2,1)S(1)} collective-permute-done((s16[272,256]{1,0:T(8,128)(2,1)S(1)}, s16[272,256]{1,0:T(8,128)(2,1)S(1)}, u32[]{:S(2)}, u32[]{:S(2)}) %collective-permute-start.27) | collective-permute-done | bytes 139296 | tf_op jit(solution)/shard_map/ppermute | solution.py:280
  108.5 1.7 %collective-permute-start.31 = (s16[272,256]{1,0:T(8,128)(2,1)S(1)}, s16[272,256]{1,0:T(8,128)(2,1)S(1)}, u32[]{:S(2)}, u32[]{:S(2)}) collective-permute-start(s16[272,256]{1,0:T(8,128)(2,1)S(1)} %finish.3.refs_0_), channel_id=1, source_target_pairs={{0,16},{8,24},{16,0},{24,8},{1,17},{9,25},{17,1},{25,9},{2,18},{10... | collective-permute-start | bytes 417800 | tf_op jit(solution)/shard_map/ppermute | solution.py:280
  112.0 2.4 %collective-permute-start.33 = (s16[1,272,256]{2,1,0:T(8,128)(2,1)S(1)}, s16[1,272,256]{2,1,0:T(8,128)(2,1)S(1)}, u32[]{:S(2)}, u32[]{:S(2)}) collective-permute-start(s16[1,272,256]{2,1,0:T(8,128)(2,1)S(1)} %get-tuple-element.99), channel_id=1, source_target_pairs={{0,4},{1,5},{2,6},{3,7},{4,0},{5,1},{6,2},{7,3},{8,12},{9,13},{10,... | collective-permute-start | bytes 417800 | tf_op jit(solution)/shard_map/ppermute | solution.py:283
  116.6 2.1 %collective-permute-start.34 = (s16[272,256]{1,0:T(8,128)(2,1)S(1)}, s16[272,256]{1,0:T(8,128)(2,1)S(1)}, u32[]{:S(2)}, u32[]{:S(2)}) collective-permute-start(s16[272,256]{1,0:T(8,128)(2,1)S(1)} %finish.4.refs_0_), channel_id=1, source_target_pairs={{0,8},{8,0},{16,24},{24,16},{1,9},{9,1},{17,25},{25,17},{2,10},{10... | collective-permute-start | bytes 417800 | tf_op jit(solution)/shard_map/ppermute | solution.py:280
  118.7 1.6 %spread.3.refs_4_ = f32[1024,768]{1,0:T(8,128)} custom-call(s32[4]{0:T(128)S(1)} %pad_add_fusion.2.order_ref.bits_ref, s16[272,256]{1,0:T(8,128)(2,1)S(1)} %finish.3.refs_0_, s16[272,256]{1,0:T(8,128)(2,1)S(1)} %collective-permute-done.30.refs_1_, s16[272,256]{1,0:T(8,128)(2,1)S(1)} %collective-permute-done.31.refs_2_, ...), custom_call_target="tpu_custom_call" | custom-call | bytes 1572864 | tf_op jit(solution)/shard_map/spread/pallas_call | solution.py:419
  120.9 2.1 %collective-permute-start.39 = (s16[272,256]{1,0:T(8,128)(2,1)S(1)}, s16[272,256]{1,0:T(8,128)(2,1)S(1)}, u32[]{:S(2)}, u32[]{:S(2)}) collective-permute-start(s16[272,256]{1,0:T(8,128)(2,1)S(1)} %finish.5.refs_0_), channel_id=1, source_target_pairs={{0,24},{8,16},{16,8},{24,0},{1,25},{9,17},{17,9},{25,1},{2,26},{10... | collective-permute-start | bytes 417800 | tf_op jit(solution)/shard_map/ppermute | solution.py:280
  124.5 1.6 %spread.4.refs_4_ = f32[1024,768]{1,0:T(8,128)} custom-call(s32[4]{0:T(128)S(1)} %pad_add_fusion.2.order_ref.bits_ref, s16[272,256]{1,0:T(8,128)(2,1)S(1)} %finish.4.refs_0_, s16[272,256]{1,0:T(8,128)(2,1)S(1)} %collective-permute-done.34.refs_1_, s16[272,256]{1,0:T(8,128)(2,1)S(1)} %collective-permute-done.35.refs_2_, ...), custom_call_target="tpu_custom_call", output_to_operand_aliasing={{}: (5, {})} | custom-call | bytes 1572864 | tf_op jit(solution)/shard_map/spread/pallas_call | solution.py:419
  128.5 1.6 %spread.5 = f32[1024,768]{1,0:T(8,128)} custom-call(s32[4]{0:T(128)S(1)} %pad_add_fusion.2.order_ref.bits_ref, s16[272,256]{1,0:T(8,128)(2,1)S(1)} %finish.5.refs_0_, s16[272,256]{1,0:T(8,128)(2,1)S(1)} %collective-permute-done.37.refs_1_, s16[272,256]{1,0:T(8,128)(2,1)S(1)} %collective-permute-done.38.refs_2_, ...), custom_call_target="tpu_custom_call", output_to_operand_aliasing={{}: (5, {})} | custom-call | bytes 1572864 | tf_op jit(solution)/shard_map/spread/pallas_call | solution.py:419
  (102 shorter events, 46.4 us)
Async XLA Ops:
  0.0 21.2 %collective-permute-start.4 = (bf16[48,256,256]{2,1,0:T(8,128)(2,1)}, bf16[48,256,256]{2,1,0:T(8,128)(2,1)}, u32[]{:S(2)}, u32[]{:S(2)}) collective-permute-start(bf16[48,256,256]{2,1,0:T(8,128)(2,1)} %tiles.1), channel_id=1, source_target_pairs={{0,1},{1,0},{2,3},{3,2},{4,5},{5,4},{6,7},{7,6},{8,9},{9,8},{10,11... | collective-permute-start | bytes 18874376 | tf_op jit(solution)/shard_map/ppermute | solution.py:277
  1.4 11.8 %collective-permute-start.3 = (bf16[512,256]{1,0:T(8,128)(2,1)S(1)}, bf16[512,256]{1,0:T(8,128)(2,1)S(1)}, u32[]{:S(2)}, u32[]{:S(2)}) collective-permute-start(bf16[512,256]{1,0:T(8,128)(2,1)S(1)} %constant_dynamic-slice_fusion.2), channel_id=1, source_target_pairs={{0,24},{8,16},{16,8},{24,0},{1,25},{9,17},{17,9},{25,1},{2,26},{10... | collective-permute-start | bytes 786440 | tf_op jit(solution)/shard_map/ppermute | solution.py:280
  4.9 12.6 %collective-permute-start.2 = (bf16[512,256]{1,0:T(8,128)(2,1)S(1)}, bf16[512,256]{1,0:T(8,128)(2,1)S(1)}, u32[]{:S(2)}, u32[]{:S(2)}) collective-permute-start(bf16[512,256]{1,0:T(8,128)(2,1)S(1)} %constant_dynamic-slice_fusion.2), channel_id=1, source_target_pairs={{0,16},{8,24},{16,0},{24,8},{1,17},{9,25},{17,1},{25,9},{2,18},{10... | collective-permute-start | bytes 786440 | tf_op jit(solution)/shard_map/ppermute | solution.py:280
  5.4 12.4 %collective-permute-start.1 = (bf16[512,256]{1,0:T(8,128)(2,1)S(1)}, bf16[512,256]{1,0:T(8,128)(2,1)S(1)}, u32[]{:S(2)}, u32[]{:S(2)}) collective-permute-start(bf16[512,256]{1,0:T(8,128)(2,1)S(1)} %constant_dynamic-slice_fusion.2), channel_id=1, source_target_pairs={{0,8},{8,0},{16,24},{24,16},{1,9},{9,1},{17,25},{25,17},{2,10},{10... | collective-permute-start | bytes 786440 | tf_op jit(solution)/shard_map/ppermute | solution.py:280
  18.9 12.8 %collective-permute-start.6 = (bf16[512,256]{1,0:T(8,128)(2,1)S(1)}, bf16[512,256]{1,0:T(8,128)(2,1)S(1)}, u32[]{:S(2)}, u32[]{:S(2)}) collective-permute-start(bf16[512,256]{1,0:T(8,128)(2,1)S(1)} %get-tuple-element.115.refs_0_), channel_id=1, source_target_pairs={{0,8},{8,0},{16,24},{24,16},{1,9},{9,1},{17,25},{25,17},{2,10},{10... | collective-permute-start | bytes 786440 | tf_op jit(solution)/shard_map/ppermute | solution.py:280
  20.5 13.2 %collective-permute-start.7 = (bf16[512,256]{1,0:T(8,128)(2,1)S(1)}, bf16[512,256]{1,0:T(8,128)(2,1)S(1)}, u32[]{:S(2)}, u32[]{:S(2)}) collective-permute-start(bf16[512,256]{1,0:T(8,128)(2,1)S(1)} %get-tuple-element.114.refs_0_), channel_id=1, source_target_pairs={{0,16},{8,24},{16,0},{24,8},{1,17},{9,25},{17,1},{25,9},{2,18},{10... | collective-permute-start | bytes 786440 | tf_op jit(solution)/shard_map/ppermute | solution.py:280
  32.2 12.9 %collective-permute-start.9 = (bf16[1024,256]{1,0:T(8,128)(2,1)S(1)}, bf16[1024,256]{1,0:T(8,128)(2,1)S(1)}, u32[]{:S(2)}, u32[]{:S(2)}) collective-permute-start(bf16[1024,256]{1,0:T(8,128)(2,1)S(1)} %join.4.refs_0_), channel_id=1, source_target_pairs={{0,16},{8,24},{16,0},{24,8},{1,17},{9,25},{17,1},{25,9},{2,18},{10... | collective-permute-start | bytes 1572872 | tf_op jit(solution)/shard_map/ppermute | solution.py:280
  34.3 12.6 %collective-permute-start.12 = (bf16[1024,256]{1,0:T(8,128)(2,1)S(1)}, bf16[1024,256]{1,0:T(8,128)(2,1)S(1)}, u32[]{:S(2)}, u32[]{:S(2)}) collective-permute-start(bf16[1024,256]{1,0:T(8,128)(2,1)S(1)} %join.5.refs_0_), channel_id=1, source_target_pairs={{0,8},{8,0},{16,24},{24,16},{1,9},{9,1},{17,25},{25,17},{2,10},{10... | collective-permute-start | bytes 1572872 | tf_op jit(solution)/shard_map/ppermute | solution.py:280
  35.4 31.7 %collective-permute-start.14 = (s16[8,272,256]{2,1,0:T(8,128)(2,1)S(1)}, s16[8,272,256]{2,1,0:T(8,128)(2,1)S(1)}, u32[]{:S(2)}, u32[]{:S(2)}) collective-permute-start(s16[8,272,256]{2,1,0:T(8,128)(2,1)S(1)} %get-tuple-element.58), channel_id=1, source_target_pairs={{0,2},{1,3},{2,0},{3,1},{4,6},{5,7},{6,4},{7,5},{8,10},{9,11},{10,... | collective-permute-start | bytes 3342344 | tf_op jit(solution)/shard_map/ppermute | solution.py:283
  35.6 11.4 %collective-permute-start.8 = (bf16[1024,256]{1,0:T(8,128)(2,1)S(1)}, bf16[1024,256]{1,0:T(8,128)(2,1)S(1)}, u32[]{:S(2)}, u32[]{:S(2)}) collective-permute-start(bf16[1024,256]{1,0:T(8,128)(2,1)S(1)} %join.4.refs_0_), channel_id=1, source_target_pairs={{0,1},{1,0},{2,3},{3,2},{4,5},{5,4},{6,7},{7,6},{8,9},{9,8},{10,11... | collective-permute-start | bytes 1572872 | tf_op jit(solution)/shard_map/ppermute | solution.py:277
  45.1 11.6 %collective-permute-start.11 = (bf16[1024,256]{1,0:T(8,128)(2,1)S(1)}, bf16[1024,256]{1,0:T(8,128)(2,1)S(1)}, u32[]{:S(2)}, u32[]{:S(2)}) collective-permute-start(bf16[1024,256]{1,0:T(8,128)(2,1)S(1)} %join.5.refs_0_), channel_id=1, source_target_pairs={{0,1},{1,0},{2,3},{3,2},{4,5},{5,4},{6,7},{7,6},{8,9},{9,8},{10,11... | collective-permute-start | bytes 1572872 | tf_op jit(solution)/shard_map/ppermute | solution.py:277
  46.9 9.8 %collective-permute-start.13 = (bf16[1024,256]{1,0:T(8,128)(2,1)S(1)}, bf16[1024,256]{1,0:T(8,128)(2,1)S(1)}, u32[]{:S(2)}, u32[]{:S(2)}) collective-permute-start(bf16[1024,256]{1,0:T(8,128)(2,1)S(1)} %collective-permute-done.12.refs_2_), channel_id=1, source_target_pairs={{0,1},{1,0},{2,3},{3,2},{4,5},{5,4},{6,7},{7,6},{8,9},{9,8},{10,11... | collective-permute-start | bytes 1572872 | tf_op jit(solution)/shard_map/ppermute | solution.py:277
  54.7 15.6 %collective-permute-start.16 = (s16[4,272,256]{2,1,0:T(8,128)(2,1)S(1)}, s16[4,272,256]{2,1,0:T(8,128)(2,1)S(1)}, u32[]{:S(2)}, u32[]{:S(2)}) collective-permute-start(s16[4,272,256]{2,1,0:T(8,128)(2,1)S(1)} %get-tuple-element.70), channel_id=1, source_target_pairs={{0,16},{8,24},{16,0},{24,8},{1,17},{9,25},{17,1},{25,9},{2,18},{10... | collective-permute-start | bytes 1671176 | tf_op jit(solution)/shard_map/ppermute | solution.py:280
  56.2 15.6 %collective-permute-start.15 = (s16[4,272,256]{2,1,0:T(8,128)(2,1)S(1)}, s16[4,272,256]{2,1,0:T(8,128)(2,1)S(1)}, u32[]{:S(2)}, u32[]{:S(2)}) collective-permute-start(s16[4,272,256]{2,1,0:T(8,128)(2,1)S(1)} %get-tuple-element.63), channel_id=1, source_target_pairs={{0,8},{8,0},{16,24},{24,16},{1,9},{9,1},{17,25},{25,17},{2,10},{10... | collective-permute-start | bytes 1671176 | tf_op jit(solution)/shard_map/ppermute | solution.py:280
  64.5 17.8 %collective-permute-start.18 = (s16[4,272,256]{2,1,0:T(8,128)(2,1)S(1)}, s16[4,272,256]{2,1,0:T(8,128)(2,1)S(1)}, u32[]{:S(2)}, u32[]{:S(2)}) collective-permute-start(s16[4,272,256]{2,1,0:T(8,128)(2,1)S(1)} %get-tuple-element.74), channel_id=1, source_target_pairs={{0,16},{8,24},{16,0},{24,8},{1,17},{9,25},{17,1},{25,9},{2,18},{10... | collective-permute-start | bytes 1671176 | tf_op jit(solution)/shard_map/ppermute | solution.py:280
  66.0 17.8 %collective-permute-start.17 = (s16[4,272,256]{2,1,0:T(8,128)(2,1)S(1)}, s16[4,272,256]{2,1,0:T(8,128)(2,1)S(1)}, u32[]{:S(2)}, u32[]{:S(2)}) collective-permute-start(s16[4,272,256]{2,1,0:T(8,128)(2,1)S(1)} %get-tuple-element.65), channel_id=1, source_target_pairs={{0,8},{8,0},{16,24},{24,16},{1,9},{9,1},{17,25},{25,17},{2,10},{10... | collective-permute-start | bytes 1671176 | tf_op jit(solution)/shard_map/ppermute | solution.py:280
  68.2 25.6 %collective-permute-start.21 = (s16[4,272,256]{2,1,0:T(8,128)(2,1)S(1)}, s16[4,272,256]{2,1,0:T(8,128)(2,1)S(1)}, u32[]{:S(2)}, u32[]{:S(2)}) collective-permute-start(s16[4,272,256]{2,1,0:T(8,128)(2,1)S(1)} %get-tuple-element.68), channel_id=1, source_target_pairs={{0,4},{1,5},{2,6},{3,7},{4,0},{5,1},{6,2},{7,3},{8,12},{9,13},{10,... | collective-permute-start | bytes 1671176 | tf_op jit(solution)/shard_map/ppermute | solution.py:283
  72.9 16.8 %collective-permute-start.20 = (s16[2,272,256]{2,1,0:T(8,128)(2,1)S(1)}, s16[2,272,256]{2,1,0:T(8,128)(2,1)S(1)}, u32[]{:S(2)}, u32[]{:S(2)}) collective-permute-start(s16[2,272,256]{2,1,0:T(8,128)(2,1)S(1)} %get-tuple-element.78), channel_id=1, source_target_pairs={{0,8},{8,0},{16,24},{24,16},{1,9},{9,1},{17,25},{25,17},{2,10},{10... | collective-permute-start | bytes 835592 | tf_op jit(solution)/shard_map/ppermute | solution.py:280
  73.5 16.2 %collective-permute-start.19 = (s16[2,272,256]{2,1,0:T(8,128)(2,1)S(1)}, s16[2,272,256]{2,1,0:T(8,128)(2,1)S(1)}, u32[]{:S(2)}, u32[]{:S(2)}) collective-permute-start(s16[2,272,256]{2,1,0:T(8,128)(2,1)S(1)} %get-tuple-element.72), channel_id=1, source_target_pairs={{0,16},{8,24},{16,0},{24,8},{1,17},{9,25},{17,1},{25,9},{2,18},{10... | collective-permute-start | bytes 835592 | tf_op jit(solution)/shard_map/ppermute | solution.py:280
  84.9 9.8 %collective-permute-start.23 = (s16[2,272,256]{2,1,0:T(8,128)(2,1)S(1)}, s16[2,272,256]{2,1,0:T(8,128)(2,1)S(1)}, u32[]{:S(2)}, u32[]{:S(2)}) collective-permute-start(s16[2,272,256]{2,1,0:T(8,128)(2,1)S(1)} %get-tuple-element.85), channel_id=1, source_target_pairs={{0,8},{8,0},{16,24},{24,16},{1,9},{9,1},{17,25},{25,17},{2,10},{10... | collective-permute-start | bytes 835592 | tf_op jit(solution)/shard_map/ppermute | solution.py:280
  90.5 9.9 %collective-permute-start.24 = (s16[2,272,256]{2,1,0:T(8,128)(2,1)S(1)}, s16[2,272,256]{2,1,0:T(8,128)(2,1)S(1)}, u32[]{:S(2)}, u32[]{:S(2)}) collective-permute-start(s16[2,272,256]{2,1,0:T(8,128)(2,1)S(1)} %get-tuple-element.80), channel_id=1, source_target_pairs={{0,2},{1,3},{2,0},{3,1},{4,6},{5,7},{6,4},{7,5},{8,10},{9,11},{10,... | collective-permute-start | bytes 835592 | tf_op jit(solution)/shard_map/ppermute | solution.py:283
  95.6 15.7 %collective-permute-start.29 = (s16[2,272,256]{2,1,0:T(8,128)(2,1)S(1)}, s16[2,272,256]{2,1,0:T(8,128)(2,1)S(1)}, u32[]{:S(2)}, u32[]{:S(2)}) collective-permute-start(s16[2,272,256]{2,1,0:T(8,128)(2,1)S(1)} %get-tuple-element.87), channel_id=1, source_target_pairs={{0,2},{1,3},{2,0},{3,1},{4,6},{5,7},{6,4},{7,5},{8,10},{9,11},{10,... | collective-permute-start | bytes 835592 | tf_op jit(solution)/shard_map/ppermute | solution.py:283
  101.2 9.4 %collective-permute-start.28 = (s16[1,272,256]{2,1,0:T(8,128)(2,1)S(1)}, s16[1,272,256]{2,1,0:T(8,128)(2,1)S(1)}, u32[]{:S(2)}, u32[]{:S(2)}) collective-permute-start(s16[1,272,256]{2,1,0:T(8,128)(2,1)S(1)} %get-tuple-element.90), channel_id=1, source_target_pairs={{0,4},{1,5},{2,6},{3,7},{4,0},{5,1},{6,2},{7,3},{8,12},{9,13},{10,... | collective-permute-start | bytes 417800 | tf_op jit(solution)/shard_map/ppermute | solution.py:283
  115.2 9.3 %collective-permute-start.35 = (s16[272,256]{1,0:T(8,128)(2,1)S(1)}, s16[272,256]{1,0:T(8,128)(2,1)S(1)}, u32[]{:S(2)}, u32[]{:S(2)}) collective-permute-start(s16[272,256]{1,0:T(8,128)(2,1)S(1)} %finish.4.refs_0_), channel_id=1, source_target_pairs={{0,16},{8,24},{16,0},{24,8},{1,17},{9,25},{17,1},{25,9},{2,18},{10... | collective-permute-start | bytes 417800 | tf_op jit(solution)/shard_map/ppermute | solution.py:280
  (21 other events, 129.8 us)
